TPU v7x, 32 devices: a whole 2x2x4 slice. The times are simulated.
32 devices in a mesh: shard: 8 (over z, y), rep: 4 (over x, core).
Axes of the slice: x: 2, y: 2, z: 4, core: 2. Of those that a mesh axis runs over, the one named last changes fastest.
Arguments:
- embeddings: bfloat16 [16384, 1024], P('shard'), may hold values from -200 to 200
- labels: int32 [16384], P('shard'), may hold values from 0 to 15, never falling along the last dimension, each value on 1 to 8193 neighbouring positions
Outputs:
- best_similarity: float32 [16384], P('shard')
Inputs may be any that keep to these rules, and one draw needn't show every extreme that they name: labels never fall along the rows; each cluster holds at most 8193 consecutive rows, and one cluster holds exactly that many.
All inputs are finite; a program needn't handle non-finite values.
Results may differ from a plain program's by a relative error of at most 0.00063.
Values may be sent and summed in bfloat16 or wider, within the bound.
No kernel may reach another device: no remote copies, remote signals or barrier semaphores. Data moves between devices by JAX's collectives and lax.ppermute only.
A program may use at most 64 MiB of HBM per device.

v0:
```python
import math

import jax
import jax.numpy as jnp
from jax import lax
from jax.sharding import PartitionSpec as P

LOOK = 4


def shifted(block, axis, distance):
    devices = range(lax.axis_size(axis))
    route = [(i - distance, i) for i in devices if i - distance in devices]
    return lax.ppermute(block, axis, route)


def normalize(values):
    as_float = values.astype(jnp.float32)
    inverse = lax.rsqrt(jnp.mean(as_float * as_float, axis=1, keepdims=True) + 1e-06)
    return (as_float * inverse / math.sqrt(values.shape[1])).astype(jnp.bfloat16)


def compare(queries, query_labels, query_pos, keys, key_labels, key_pos, current):
    scores = lax.dot_general(
        queries, keys, (((1,), (1,)), ((), ())), preferred_element_type=jnp.float32
    )
    keep = (key_labels[None, :] == query_labels[:, None]) & (key_pos[None, :] < query_pos[:, None])
    return jnp.maximum(current, jnp.max(jnp.where(keep, scores, jnp.float32(-1.0)), axis=1))


def fetch(sent_piece, offset_dev):
    result = shifted((sent_piece[0], sent_piece[1]), "shard", offset_dev)
    return result


def local(embeddings, labels):
    tok_rows = embeddings.shape[0]
    rep_count = lax.axis_size("rep")
    device = lax.axis_index("shard")
    replica = lax.axis_index("rep")
    unit_rows = normalize(embeddings)
    positions = device * tok_rows + jnp.arange(tok_rows, dtype=jnp.int32)
    quarter = tok_rows // rep_count
    start_row = replica * quarter
    queries, query_labels, query_pos = (unit_rows, labels, positions)
    sent_piece = (
        lax.dynamic_slice_in_dim(unit_rows, start_row, quarter, 0),
        lax.dynamic_slice_in_dim(labels, start_row, quarter, 0),
    )
    offsets = start_row + jnp.arange(quarter, dtype=jnp.int32)
    best_sim = jnp.full((queries.shape[0],), -1.0, jnp.float32)
    best_sim = compare(
        queries,
        query_labels,
        query_pos,
        sent_piece[0],
        sent_piece[1],
        device * tok_rows + offsets,
        best_sim,
    )
    carried = sent_piece
    for offset_dev in range(1, LOOK + 1):
        carried = fetch(sent_piece, offset_dev)
        key_pos = (device - offset_dev) * tok_rows + offsets
        key_pos = jnp.where(device >= offset_dev, key_pos, jnp.int32(2**30))
        best_sim = compare(
            queries, query_labels, query_pos, carried[0], carried[1], key_pos, best_sim
        )
    merged = lax.pmax(best_sim, "rep")
    return merged


def solution(mesh):
    placed = (P("shard", None), P("shard"))
    return jax.shard_map(local, mesh=mesh, in_specs=placed, out_specs=P("shard"), check_vma=False)
```

profile of v0, /device:TPU:18, one launch (start us, length us, event | category | flops | bytes accessed | tf_op | source)
XLA Modules:
  0.0 169.6 jit_solution(11547176139472006884)
XLA Ops:
  0.0 0.9 dynamic_slice.6
  0.9 1.4 collective-permute-start.6
  2.3 4.4 %collective-permute-start.4 = (s32[512]{0:T(512)S(1)}, s32[512]{0:T(512)S(1)}, u32[]{:S(2)}, u32[]{:S(2)}) collective-permute-start(s32[512]{0:T(512)S(1)} %dynamic_slice.6), channel_id=1, source_target_pairs={{0,12},{4,16},{8,20},{12,24},{16,28},{1,13},{5,17},{9,21},{13,25},... | collective-permute-start | bytes 6152 | tf_op jit(solution)/shard_map/ppermute | solution.py:14
  6.8 1.9 %collective-permute-start.2 = (s32[512]{0:T(512)S(1)}, s32[512]{0:T(512)S(1)}, u32[]{:S(2)}, u32[]{:S(2)}) collective-permute-start(s32[512]{0:T(512)S(1)} %dynamic_slice.6), channel_id=1, source_target_pairs={{0,8},{4,12},{8,16},{12,20},{16,24},{20,28},{1,9},{5,13},{9,17},{1... | collective-permute-start | bytes 6152 | tf_op jit(solution)/shard_map/ppermute | solution.py:14
  8.7 3.1 %fusion = f32[2048]{0:T(1024)S(1)} fusion(bf16[2048,1024]{1,0:T(8,128)(2,1)} %param.2), kind=kLoop, calls=%fused_computation.2 | loop fusion | flops 6289408 | bytes 4202496 | tf_op jit(solution)/shard_map/reduce_sum | solution.py:19
  11.8 0.0 copy-start.3
  11.8 1.1 fusion.2
  13.0 1.9 %copy-done.1 = bf16[2048,1024]{1,0:T(8,128)(2,1)} copy-done((bf16[2048,1024]{1,0:T(8,128)(2,1)}, bf16[2048,1024]{1,0:T(8,128)(2,1)S(1)}, u32[]{:S(2)}) %copy-start.1) | copy-done | bytes 4194328
  14.9 0.1 constant_dynamic-slice_fusion
  15.0 1.9 %collective-permute-start.5 = (bf16[512,1024]{1,0:T(8,128)(2,1)S(1)}, bf16[512,1024]{1,0:T(8,128)(2,1)S(1)}, u32[]{:S(2)}, u32[]{:S(2)}) collective-permute-start(bf16[512,1024]{1,0:T(8,128)(2,1)S(1)} %constant_dynamic-slice_fusion), channel_id=1, source_target_pairs={{0,12},{4,16},{8,20},{12,24},{16,28},{1,13},{5,17},{9,21},{13,25},... | collective-permute-start | bytes 3145736 | tf_op jit(solution)/shard_map/ppermute | solution.py:14
  16.9 1.9 %collective-permute-start.3 = (bf16[512,1024]{1,0:T(8,128)(2,1)S(1)}, bf16[512,1024]{1,0:T(8,128)(2,1)S(1)}, u32[]{:S(2)}, u32[]{:S(2)}) collective-permute-start(bf16[512,1024]{1,0:T(8,128)(2,1)S(1)} %constant_dynamic-slice_fusion), channel_id=1, source_target_pairs={{0,8},{4,12},{8,16},{12,20},{16,24},{20,28},{1,9},{5,13},{9,17},{1... | collective-permute-start | bytes 3145736 | tf_op jit(solution)/shard_map/ppermute | solution.py:14
  18.9 4.9 %select_reduce_fusion.4 = f32[2048]{0:T(1024)S(1)} fusion(bf16[2048,1024]{1,0:T(8,128)(2,1)} %copy-done.1, bf16[512,1024]{1,0:T(8,128)(2,1)S(1)} %constant_dynamic-slice_fusion, s32[2048]{0:T(1024)S(1)} %iota_add_fusion, s32[2048]{0:T(1024)S(1)} %copy-done.3, s32[512]{0:T(512)S(1)} %fusion.3, s32[512]{0:T(512)S(1)} %dynamic_slice.6), kind=kOutput, calls=%fused_computation.9 | convolution fusion | flops 2152724480 | bytes 5271552 | tf_op jit(solution)/shard_map/dot_general | solution.py:24
  23.8 39.5 %collective-permute-done.3 = bf16[512,1024]{1,0:T(8,128)(2,1)S(1)} collective-permute-done((bf16[512,1024]{1,0:T(8,128)(2,1)S(1)}, bf16[512,1024]{1,0:T(8,128)(2,1)S(1)}, u32[]{:S(2)}, u32[]{:S(2)}) %collective-permute-start.3) | collective-permute-done | bytes 1048608 | tf_op jit(solution)/shard_map/ppermute | solution.py:14
  63.3 1.3 collective-permute-start.7
  64.6 2.4 %fusion.4 = f32[2048,512]{0,1:T(8,128)S(1)} fusion(bf16[2048,1024]{1,0:T(8,128)(2,1)S(1)} %copy-done.2, bf16[512,1024]{1,0:T(8,128)(2,1)S(1)} %collective-permute-done.3), kind=kOutput, calls=%fused_computation.20 | convolution fusion | flops 2147483648 | bytes 9437184 | tf_op jit(solution)/shard_map/dot_general | solution.py:24
  67.0 0.0 collective-permute-done.5
  67.0 26.0 %collective-permute-start.1 = (bf16[512,1024]{1,0:T(8,128)(2,1)S(1)}, bf16[512,1024]{1,0:T(8,128)(2,1)S(1)}, u32[]{:S(2)}, u32[]{:S(2)}) collective-permute-start(bf16[512,1024]{1,0:T(8,128)(2,1)S(1)} %constant_dynamic-slice_fusion), channel_id=1, source_target_pairs={{0,4},{4,8},{8,12},{12,16},{16,20},{20,24},{24,28},{1,5},{5,9},{9,... | collective-permute-start | bytes 3145736 | tf_op jit(solution)/shard_map/ppermute | solution.py:14
  93.0 2.4 %fusion.5 = f32[2048,512]{0,1:T(8,128)S(1)} fusion(bf16[2048,1024]{1,0:T(8,128)(2,1)S(1)} %copy-done.2, bf16[512,1024]{1,0:T(8,128)(2,1)S(1)} %collective-permute-done.5), kind=kOutput, calls=%fused_computation.21 | convolution fusion | flops 2147483648 | bytes 9437184 | tf_op jit(solution)/shard_map/dot_general | solution.py:24
  95.4 22.9 %collective-permute-start = (s32[512]{0:T(512)S(1)}, s32[512]{0:T(512)S(1)}, u32[]{:S(2)}, u32[]{:S(2)}) collective-permute-start(s32[512]{0:T(512)S(1)} %dynamic_slice.6), channel_id=1, source_target_pairs={{0,4},{4,8},{8,12},{12,16},{16,20},{20,24},{24,28},{1,5},{5,9},{9,... | collective-permute-start | bytes 6152 | tf_op jit(solution)/shard_map/ppermute | solution.py:14
  118.3 2.4 %fusion.6 = f32[2048,512]{0,1:T(8,128)S(1)} fusion(bf16[2048,1024]{1,0:T(8,128)(2,1)S(1)} %copy-done.2, bf16[512,1024]{1,0:T(8,128)(2,1)S(1)} %collective-permute-done.7), kind=kOutput, calls=%fused_computation.22 | convolution fusion | flops 2147483648 | bytes 9437184 | tf_op jit(solution)/shard_map/dot_general | solution.py:24
  120.7 0.0 collective-permute-done.6
  120.7 34.2 %collective-permute-done = s32[512]{0:T(512)S(1)} collective-permute-done((s32[512]{0:T(512)S(1)}, s32[512]{0:T(512)S(1)}, u32[]{:S(2)}, u32[]{:S(2)}) %collective-permute-start) | collective-permute-done | bytes 2080 | tf_op jit(solution)/shard_map/ppermute | solution.py:14
  155.0 8.0 %select_reduce_fusion.3 = (f32[2048]{0:T(1024)S(1)}, f32[2048]{0:T(1024)S(1)}, f32[2048]{0:T(1024)S(1)}, f32[2048]{0:T(1024)S(1)}) fusion(s32[2048]{0:T(1024)S(1)} %iota_add_fusion, s32[2048]{0:T(1024)S(1)} %copy-done.3, s32[512]{0:T(512)S(1)} %get-tuple-element.12, s32[512]{0:T(512)S(1)} %collective-permute-done, f32[2048,512]{0,1:T(8,128)S(1)} %fusion.4, ...), kind=kOutput, calls=%fused_computation.8 | convolution fusion | flops 2168446976 | bytes 17891328 | tf_op jit(solution)/shard_map/dot_general | solution.py:24
  163.0 6.6 %pmax.7 = f32[2048]{0:T(1024)} all-reduce(f32[2048]{0:T(1024)S(1)} %maximum_maximum_fusion), channel_id=1, replica_groups=mesh['shard'=8,'rep'=4] {'rep'}, use_global_device_ids=true, to_apply=%region_6.7 | all-reduce | flops 2048 | bytes 16384 | tf_op jit(solution)/shard_map/pmax | solution.py:69
  (16 shorter events, 0.1 us)
Async XLA Ops:
  0.0 11.8 %copy-start = (bf16[2048,1024]{1,0:T(8,128)(2,1)S(1)}, bf16[2048,1024]{1,0:T(8,128)(2,1)}, u32[]{:S(2)}) copy-start(bf16[2048,1024]{1,0:T(8,128)(2,1)} %param.2) | copy-start | bytes 12582916
  0.9 119.8 %collective-permute-start.6 = (s32[512]{0:T(512)S(1)}, s32[512]{0:T(512)S(1)}, u32[]{:S(2)}, u32[]{:S(2)}) collective-permute-start(s32[512]{0:T(512)S(1)} %dynamic_slice.6), channel_id=1, source_target_pairs={{0,16},{4,20},{8,24},{12,28},{1,17},{5,21},{9,25},{13,29},{2,18},{... | collective-permute-start | bytes 6152 | tf_op jit(solution)/shard_map/ppermute | solution.py:14
  2.3 118.4 %collective-permute-start.4 = (s32[512]{0:T(512)S(1)}, s32[512]{0:T(512)S(1)}, u32[]{:S(2)}, u32[]{:S(2)}) collective-permute-start(s32[512]{0:T(512)S(1)} %dynamic_slice.6), channel_id=1, source_target_pairs={{0,12},{4,16},{8,20},{12,24},{16,28},{1,13},{5,17},{9,21},{13,25},... | collective-permute-start | bytes 6152 | tf_op jit(solution)/shard_map/ppermute | solution.py:14
  6.8 114.0 %collective-permute-start.2 = (s32[512]{0:T(512)S(1)}, s32[512]{0:T(512)S(1)}, u32[]{:S(2)}, u32[]{:S(2)}) collective-permute-start(s32[512]{0:T(512)S(1)} %dynamic_slice.6), channel_id=1, source_target_pairs={{0,8},{4,12},{8,16},{12,20},{16,24},{20,28},{1,9},{5,13},{9,17},{1... | collective-permute-start | bytes 6152 | tf_op jit(solution)/shard_map/ppermute | solution.py:14
  11.8 7.1 %copy-start.3 = (s32[2048]{0:T(1024)S(1)}, s32[2048]{0:T(1024)}, u32[]{:S(2)}) copy-start(s32[2048]{0:T(1024)} %param.3) | copy-start | bytes 24580
  13.0 1.9 %copy-start.1 = (bf16[2048,1024]{1,0:T(8,128)(2,1)}, bf16[2048,1024]{1,0:T(8,128)(2,1)S(1)}, u32[]{:S(2)}) copy-start(bf16[2048,1024]{1,0:T(8,128)(2,1)S(1)} %fusion.2) | copy-start | bytes 12582916
  15.0 52.0 %collective-permute-start.5 = (bf16[512,1024]{1,0:T(8,128)(2,1)S(1)}, bf16[512,1024]{1,0:T(8,128)(2,1)S(1)}, u32[]{:S(2)}, u32[]{:S(2)}) collective-permute-start(bf16[512,1024]{1,0:T(8,128)(2,1)S(1)} %constant_dynamic-slice_fusion), channel_id=1, source_target_pairs={{0,12},{4,16},{8,20},{12,24},{16,28},{1,13},{5,17},{9,21},{13,25},... | collective-permute-start | bytes 3145736 | tf_op jit(solution)/shard_map/ppermute | solution.py:14
  16.9 46.4 %collective-permute-start.3 = (bf16[512,1024]{1,0:T(8,128)(2,1)S(1)}, bf16[512,1024]{1,0:T(8,128)(2,1)S(1)}, u32[]{:S(2)}, u32[]{:S(2)}) collective-permute-start(bf16[512,1024]{1,0:T(8,128)(2,1)S(1)} %constant_dynamic-slice_fusion), channel_id=1, source_target_pairs={{0,8},{4,12},{8,16},{12,20},{16,24},{20,28},{1,9},{5,13},{9,17},{1... | collective-permute-start | bytes 3145736 | tf_op jit(solution)/shard_map/ppermute | solution.py:14
  18.9 45.7 %copy-start.2 = (bf16[2048,1024]{1,0:T(8,128)(2,1)S(1)}, bf16[2048,1024]{1,0:T(8,128)(2,1)}, u32[]{:S(2)}) copy-start(bf16[2048,1024]{1,0:T(8,128)(2,1)} %copy-done.1) | copy-start | bytes 12582916
  63.3 32.1 %collective-permute-start.7 = (bf16[512,1024]{1,0:T(8,128)(2,1)S(1)}, bf16[512,1024]{1,0:T(8,128)(2,1)S(1)}, u32[]{:S(2)}, u32[]{:S(2)}) collective-permute-start(bf16[512,1024]{1,0:T(8,128)(2,1)S(1)} %constant_dynamic-slice_fusion), channel_id=1, source_target_pairs={{0,16},{4,20},{8,24},{12,28},{1,17},{5,21},{9,25},{13,29},{2,18},{... | collective-permute-start | bytes 3145736 | tf_op jit(solution)/shard_map/ppermute | solution.py:14
  67.0 88.0 %collective-permute-start.1 = (bf16[512,1024]{1,0:T(8,128)(2,1)S(1)}, bf16[512,1024]{1,0:T(8,128)(2,1)S(1)}, u32[]{:S(2)}, u32[]{:S(2)}) collective-permute-start(bf16[512,1024]{1,0:T(8,128)(2,1)S(1)} %constant_dynamic-slice_fusion), channel_id=1, source_target_pairs={{0,4},{4,8},{8,12},{12,16},{16,20},{20,24},{24,28},{1,5},{5,9},{9,... | collective-permute-start | bytes 3145736 | tf_op jit(solution)/shard_map/ppermute | solution.py:14
  95.4 59.6 %collective-permute-start = (s32[512]{0:T(512)S(1)}, s32[512]{0:T(512)S(1)}, u32[]{:S(2)}, u32[]{:S(2)}) collective-permute-start(s32[512]{0:T(512)S(1)} %dynamic_slice.6), channel_id=1, source_target_pairs={{0,4},{4,8},{8,12},{12,16},{16,20},{20,24},{24,28},{1,5},{5,9},{9,... | collective-permute-start | bytes 6152 | tf_op jit(solution)/shard_map/ppermute | solution.py:14
where the time goes:
time: 170 us
  waiting for transfers between devices  73.8 us (43%)
  starting transfers between devices  61.8 us (36%)
  matrix products  20 us (12%)
  blocking collectives  6.61 us (4%)
  other arithmetic  4.24 us (2%)
  local copies, waits for them, and re-layouts  2.91 us (2%)
    ppermute x8, waiting for transfers between devices, shifted(): return lax.ppermute(block, axis, route)  73.8 us
    ppermute x8, starting transfers between devices, shifted(): return lax.ppermute(block, axis, route)  61.8 us
    dot_general x5, matrix products, compare(): lax.dot_general(queries, keys, (((1,), (1,)), ((), ())), preferred_elemen...  20 us
    pmax x1, blocking collectives, local(): merged = lax.pmax(best_sim, 'rep')  6.61 us
  transfers between devices with their start and end apart: 8, of which 2 were waited for; matrix products, arithmetic and copies ran while one was open for 10% of the time, Pallas kernels for 0%

commit v1 on v0

v1 whole, which is shorter than its diff:
```python
import functools
import math

import jax
import jax.numpy as jnp
from jax import lax
from jax.experimental import pallas as pl
from jax.experimental.pallas import tpu as pltpu
from jax.sharding import PartitionSpec as P

F32 = jnp.float32
TILE_Q = 512
TILE_K = 256
VMEM_LIMIT = 48 * 1024 * 1024


def normalize(values):
    as_float = values.astype(F32)
    inverse = lax.rsqrt(jnp.mean(as_float * as_float, axis=1, keepdims=True) + 1e-06)
    return (as_float * inverse / math.sqrt(values.shape[1])).astype(jnp.bfloat16)


def score(keys, queries):
    return lax.dot_general(keys, queries, (((1,), (1,)), ((), ())), preferred_element_type=F32)


def fold(values):
    rows, cols = values.shape
    return jnp.max(values.reshape(rows // 8, 8, cols), axis=0)


def rectangle(keys_ref, queries_ref, out_ref, first_key, query_count):
    tiles = keys_ref.shape[0] // TILE_K

    def over_queries(j, _):
        cols = pl.ds(pl.multiple_of(j * TILE_Q, TILE_Q), TILE_Q)
        queries = queries_ref[cols, :]

        def over_keys(i, best):
            keys = keys_ref[pl.ds(pl.multiple_of(i * TILE_K, TILE_K), TILE_K), :]
            scores = score(keys, queries)
            row = lax.broadcasted_iota(jnp.int32, scores.shape, 0) + i * TILE_K
            return jnp.maximum(best, fold(jnp.where(row >= first_key, scores, -1.0)))

        best = lax.fori_loop(
            first_key // TILE_K, tiles, over_keys, jnp.full((8, TILE_Q), -1.0, F32)
        )
        best = jnp.max(best, axis=0, keepdims=True)
        col = lax.broadcasted_iota(jnp.int32, best.shape, 1) + j * TILE_Q
        out_ref[:, cols] = jnp.maximum(
            out_ref[:, cols], jnp.where(col < query_count, best, -1.0)
        )
        return 0

    lax.fori_loop(0, pl.cdiv(query_count, TILE_Q), over_queries, 0)


def diagonal_kernel(tiles_ref, start_ref, own_ref, out_ref):
    rows = own_ref.shape[0]
    out_ref[...] = jnp.full(out_ref.shape, -1.0, F32)
    for n in range(tiles_ref.shape[0]):
        tile = tiles_ref[n]
        keys = own_ref[pl.ds(pl.multiple_of(tile * TILE_K, TILE_K), TILE_K), :]

        def over_queries(j, _):
            cols = pl.ds(pl.multiple_of(j * TILE_Q, TILE_Q), TILE_Q)
            scores = score(keys, own_ref[cols, :])
            row = lax.broadcasted_iota(jnp.int32, scores.shape, 0) + tile * TILE_K
            col = lax.broadcasted_iota(jnp.int32, scores.shape, 1) + j * TILE_Q
            keep = (row >= start_ref[:, cols]) & (row < col)
            best = jnp.max(fold(jnp.where(keep, scores, -1.0)), axis=0, keepdims=True)
            out_ref[:, cols] = jnp.maximum(out_ref[:, cols], best)
            return 0

        lax.fori_loop(tile * TILE_K // TILE_Q, rows // TILE_Q, over_queries, 0)


def tasks_kernel(tasks, outs, bounds_ref, *refs):
    ins, results = refs[: len(refs) - outs], refs[len(refs) - outs :]
    for result in results:
        result[...] = jnp.full(result.shape, -1.0, F32)
    for n, (keys, queries, result) in enumerate(tasks):
        rectangle(ins[keys], ins[queries], results[result], bounds_ref[2 * n], bounds_ref[2 * n + 1])


def run_tasks(name, tasks, bounds, arrays, widths):
    vmem, smem = pl.BlockSpec(memory_space=pltpu.VMEM), pl.BlockSpec(memory_space=pltpu.SMEM)
    work = sum(arrays[k].shape[0] * arrays[q].shape[0] for k, q, _ in tasks)
    return pl.pallas_call(
        functools.partial(tasks_kernel, tasks, len(widths)),
        out_shape=[jax.ShapeDtypeStruct((1, width), F32) for width in widths],
        in_specs=[smem] + [vmem] * len(arrays),
        out_specs=[vmem] * len(widths),
        compiler_params=pltpu.CompilerParams(vmem_limit_bytes=VMEM_LIMIT),
        cost_estimate=pl.CostEstimate(
            flops=2 * work * arrays[0].shape[1],
            bytes_accessed=sum(a.size * 2 for a in arrays),
            transcendentals=0,
        ),
        name=name,
    )(bounds, *arrays)


def local(embeddings, labels):
    rows = embeddings.shape[0]
    shards, reps = lax.axis_size("shard"), lax.axis_size("rep")
    s, r = lax.axis_index("shard"), lax.axis_index("rep")
    odd = s % 2
    quarter = rows // reps

    def along_shard(block, distance, keep=lambda i: True):
        route = [
            (i, i + distance) for i in range(shards) if i + distance in range(shards) and keep(i)
        ]
        return lax.ppermute(block, "shard", route)

    def partner(block):
        return lax.ppermute(block, "shard", [(i, i ^ 1) for i in range(shards)])

    def other_rep(block, flip):
        return lax.ppermute(block, "rep", [(i, i ^ flip) for i in range(reps)])

    def piece(index):
        return normalize(lax.dynamic_slice_in_dim(embeddings, index * quarter, quarter, 0))

    mine = piece(r)
    half = quarter // 2
    low_a = along_shard(mine[:half], 2)
    low_b = along_shard(mine[half:], 2)
    high = along_shard(mine, -2)
    across = partner(piece(jnp.where(odd == 1, r, r ^ 2)))
    across_index = jnp.where(odd == 1, r ^ 2, r)

    first, last = labels[0], labels[-1]
    head = jnp.sum((labels == first).astype(jnp.int32))
    tail = jnp.sum((labels == last).astype(jnp.int32))
    info = lax.all_gather(jnp.stack([first, last, head, tail]), "shard")

    def bounds(query_shard, key_shard, key_piece, query_offset, query_rows, enabled=True):
        valid = (query_shard < shards) & (key_shard >= 0) & enabled
        query_info = info[jnp.clip(query_shard, 0, shards - 1)]
        key_info = info[jnp.clip(key_shard, 0, shards - 1)]
        valid &= query_info[0] == key_info[1]
        first_key = jnp.clip(rows - key_info[3] - key_piece * quarter, 0, quarter)
        count = jnp.clip(query_info[2] - query_offset, 0, query_rows)
        return [first_key, jnp.where(valid & (first_key < quarter), count, 0)]

    def packed(*pairs):
        return jnp.stack([value for pair in pairs for value in pair]).astype(jnp.int32)

    own = normalize(embeddings)
    index = jnp.arange(rows, dtype=jnp.int32)
    begins = jnp.concatenate([jnp.ones((1,), jnp.bool_), labels[1:] != labels[:-1]])
    start = lax.cummax(jnp.where(begins, index, 0))
    tiles_each = rows // TILE_K // reps
    numbers = [
        r + n * reps if n % 2 == 0 else (n + 1) * reps - 1 - r for n in range(tiles_each)
    ]
    vmem, smem = pl.BlockSpec(memory_space=pltpu.VMEM), pl.BlockSpec(memory_space=pltpu.SMEM)
    best = pl.pallas_call(
        diagonal_kernel,
        out_shape=jax.ShapeDtypeStruct((1, rows), F32),
        in_specs=[smem, vmem, vmem],
        out_specs=vmem,
        compiler_params=pltpu.CompilerParams(vmem_limit_bytes=VMEM_LIMIT),
        cost_estimate=pl.CostEstimate(
            flops=rows * rows * embeddings.shape[1] // reps,
            bytes_accessed=rows * embeddings.shape[1] * 2,
            transcendentals=0,
        ),
        name="diagonal",
    )(jnp.stack(numbers).astype(jnp.int32), start[None, :], own)

    low = jnp.concatenate([low_a, low_b], axis=0)
    across_2 = other_rep(across, 1)
    a0, a1 = across_index, across_index ^ 1
    near = run_tasks(
        "near",
        [(0, 1, 0), (2, 1, 0), (0, 2, 1), (0, 3, 2), (2, 4, 3), (3, 4, 3)],
        packed(
            bounds(s, s - 2, r, 0, rows),
            bounds(s, s - 1, a0, 0, rows, odd == 1),
            bounds(s ^ 1, s - 2, r, a0 * quarter, quarter),
            bounds(s ^ 1, s - 2, r, a1 * quarter, quarter),
            bounds(s + 2, s ^ 1, a0, r * quarter, quarter),
            bounds(s + 2, s ^ 1, a1, r * quarter, quarter),
        ),
        [low, own, across, across_2, high],
        [rows, quarter, quarter, quarter],
    )
    from_partner = [partner(near[1][0]), partner(near[2][0])]

    even_only = lambda i: i % 2 == 0
    high_across = along_shard(high, 1, even_only)
    low_1 = other_rep(low, 1)
    low_2a, low_2b = other_rep(low_a, 2), other_rep(low_b, 2)
    low_2 = jnp.concatenate([low_2a, low_2b], axis=0)
    low_3 = other_rep(low_2, 1)
    far = run_tasks(
        "far",
        [(n, 4, 0) for n in range(4)] + [(n, 5, 1) for n in range(4)],
        packed(
            *[bounds(s + 2, s - 2, r ^ n, r * quarter, quarter) for n in range(4)],
            *[bounds(s + 1, s - 2, r ^ n, r * quarter, quarter, odd == 1) for n in range(4)],
        ),
        [low, low_1, low_2, low_3, high, high_across],
        [quarter, quarter],
    )

    above = along_shard(jnp.maximum(near[3][0], far[0][0]), 2)
    above = jnp.where(s >= 2, above, -1.0)
    across_above = along_shard(far[1][0], 1, lambda i: i % 2 == 1)
    across_above = jnp.where((s >= 2) & (odd == 0), across_above, -1.0)

    def placed(values, index):
        return lax.dynamic_update_slice_in_dim(
            jnp.full((rows,), -1.0, F32), values, index * quarter, 0
        )

    home = jnp.where(odd == 1, r, r ^ 2)
    best = jnp.maximum(best[0], near[0][0])
    best = jnp.maximum(best, placed(from_partner[0], home))
    best = jnp.maximum(best, placed(from_partner[1], home ^ 1))
    best = jnp.maximum(best, placed(jnp.maximum(above, across_above), r))
    return lax.pmax(best, "rep")


def solution(mesh):
    placed = (P("shard", None), P("shard"))
    return jax.shard_map(local, mesh=mesh, in_specs=placed, out_specs=P("shard"), check_vma=False)
```

time: 170 us -> 136 us (0.80)
  the two profiles are of different devices: /device:TPU:18 before, /device:TPU:8 now
where the time goes in v1:
time: 136 us; the launch traced here: 134 us
  starting transfers between devices  38.5 us (28%)
  blocking collectives  24.6 us (18%)
  waiting for transfers between devices  20.7 us (15%)
  other arithmetic  18 us (13%)
  between operations  13.6 us (10%)
  Pallas kernels  9.77 us (7%)
  local copies, waits for them, and re-layouts  8.63 us (6%)
    ppermute x6, starting transfers between devices, along_shard(): return lax.ppermute(block, 'shard', route)  21.8 us
    unnamed x1, blocking collectives  18.1 us
    ppermute x5, waiting for transfers between devices, other_rep(): return lax.ppermute(block, 'rep', [(i, i ^ flip) for i in range(reps)])  16.2 us
    ppermute x3, starting transfers between devices, partner(): return lax.ppermute(block, 'shard', [(i, i ^ 1) for i in range(shards)])  14.3 us
    convert_element_type x2, other arithmetic, normalize(): (as_float * inverse / math.sqrt(values.shape[1])).astype(jnp.bfloat16)  7.52 us
    pallas_call x2, Pallas kernels, run_tasks(): pl.pallas_call(functools.partial(tasks_kernel, tasks, len(widths)), out_s...  6.61 us
    pmax x1, blocking collectives, local(): return lax.pmax(best, 'rep')  6.44 us
    reduce_sum x2, other arithmetic, normalize(): jnp.mean(as_float * as_float, axis=1, keepdims=True) + 1e-06  5.09 us
  transfers between devices with their start and end apart: 14, of which 4 were waited for; matrix products, arithmetic and copies ran while one was open for 16% of the time, Pallas kernels for 7%

profile of v1, /device:TPU:8, one launch (start us, length us, event | category | flops | bytes accessed | tf_op | source)
XLA Modules:
  0.0 133.8 jit_solution(6608018423301685836)
XLA Ops:
  0.0 2.0 %fusion.6 = (f32[512]{0:T(512)S(1)}, f32[512]{0:T(512)S(1)}) fusion(bf16[2048,1024]{1,0:T(8,128)(2,1)} %param.2, s32[]{:T(128)S(6)} %select_n.126, s32[]{:T(128)S(6)} %select_n.124), kind=kLoop, calls=%fused_computation.12 | loop fusion | flops 3144704 | bytes 2101256 | tf_op jit(solution)/shard_map/reduce_sum | solution.py:19
  2.0 3.5 %fusion.8 = (bf16[512,1024]{1,0:T(8,128)(2,1)}, bf16[512,1024]{1,0:T(8,128)(2,1)}) fusion(f32[512]{0:T(512)S(1)} %get-tuple-element.53, bf16[2048,1024]{1,0:T(8,128)(2,1)} %param.2, s32[]{:T(128)S(6)} %select_n.126, f32[512]{0:T(512)S(1)} %get-tuple-element.54, s32[]{:T(128)S(6)} %select_n.124), kind=kLoop, calls=%fused_computation.14 | loop fusion | flops 4194304 | bytes 4198408 | tf_op jit(solution)/shard_map/convert_element_type | solution.py:20
  5.5 2.0 %collective-permute-start.4 = (bf16[512,1024]{1,0:T(8,128)(2,1)}, bf16[512,1024]{1,0:T(8,128)(2,1)S(1)}, u32[]{:S(2)}, u32[]{:S(2)}) collective-permute-start(bf16[512,1024]{1,0:T(8,128)(2,1)} %get-tuple-element.22), channel_id=1, source_target_pairs={{8,0},{12,4},{16,8},{20,12},{24,16},{28,20},{9,1},{13,5},{17,9},{2... | collective-permute-start | bytes 3145736 | tf_op jit(solution)/shard_map/ppermute | solution.py:115
  7.5 1.3 fusion.9
  8.8 3.9 %collective-permute-start = (bf16[256,1024]{1,0:T(8,128)(2,1)S(1)}, bf16[256,1024]{1,0:T(8,128)(2,1)S(1)}, u32[]{:S(2)}, u32[]{:S(2)}) collective-permute-start(bf16[256,1024]{1,0:T(8,128)(2,1)S(1)} %get-tuple-element.24), channel_id=1, source_target_pairs={{0,8},{4,12},{8,16},{12,20},{16,24},{20,28},{1,9},{5,13},{9,17},{1... | collective-permute-start | bytes 1572872 | tf_op jit(solution)/shard_map/ppermute | solution.py:115
  12.8 3.5 %collective-permute-start.1 = (bf16[256,1024]{1,0:T(8,128)(2,1)S(1)}, bf16[256,1024]{1,0:T(8,128)(2,1)}, u32[]{:S(2)}, u32[]{:S(2)}) collective-permute-start(bf16[256,1024]{1,0:T(8,128)(2,1)S(1)} %get-tuple-element.23), channel_id=1, source_target_pairs={{0,8},{4,12},{8,16},{12,20},{16,24},{20,28},{1,9},{5,13},{9,17},{1... | collective-permute-start | bytes 1572872 | tf_op jit(solution)/shard_map/ppermute | solution.py:115
  16.3 1.7 %collective-permute-start.2 = (bf16[512,1024]{1,0:T(8,128)(2,1)}, bf16[512,1024]{1,0:T(8,128)(2,1)}, u32[]{:S(2)}, u32[]{:S(2)}) collective-permute-start(bf16[512,1024]{1,0:T(8,128)(2,1)} %get-tuple-element.21), channel_id=1, source_target_pairs={{0,4},{4,0},{8,12},{12,8},{16,20},{20,16},{24,28},{28,24},{1,5},{5... | collective-permute-start | bytes 3145736 | tf_op jit(solution)/shard_map/ppermute | solution.py:118
  18.0 3.1 %fusion = f32[2048]{0:T(1024)S(1)} fusion(bf16[2048,1024]{1,0:T(8,128)(2,1)} %param.2), kind=kLoop, calls=%fused_computation.2 | loop fusion | flops 6289408 | bytes 4202496 | tf_op jit(solution)/shard_map/reduce_sum | solution.py:19
  23.0 1.9 %convert_reduce_fusion.1 = (s32[]{:T(128)}, s32[]{:T(128)}) fusion(s32[2048]{0:T(1024)S(1)} %copy-done.1, s32[]{:T(128)} %bitcast.4, s32[]{:T(128)} %bitcast.6), kind=kLoop, calls=%fused_computation.22 | loop fusion | flops 12286 | bytes 8208 | tf_op jit(solution)/shard_map/reduce_sum | solution.py:135
  25.0 2.6 %add_dynamic-update-slice_fusion = s32[32]{0:T(128)S(1)} fusion(s32[32]{0:T(128)S(1)} %broadcast.62, u32[]{:T(128)} %bitcast.8, s32[1]{0:T(128)} %bitcast.7, s32[1]{0:T(128)} %bitcast.5, s32[1]{0:T(128)} %get-tuple-element.25, s32[1]{0:T(128)} %get-tuple-element.26), kind=kLoop, calls=%fused_computation.38 | loop fusion | flops 12 | bytes 148
  27.6 18.1 %all-reduce = s32[32]{0:T(128)S(1)} all-reduce(s32[32]{0:T(128)S(1)} %add_dynamic-update-slice_fusion), channel_id=2, replica_groups=mesh['shard'=8,'rep'=4] {'shard'}, use_global_device_ids=true, to_apply=%add | all-reduce | flops 32 | bytes 256
  46.6 1.5 %collective-permute-start.8 = (bf16[256,1024]{1,0:T(8,128)(2,1)S(1)}, bf16[256,1024]{1,0:T(8,128)(2,1)}, u32[]{:S(2)}, u32[]{:S(2)}) collective-permute-start(bf16[256,1024]{1,0:T(8,128)(2,1)S(1)} %collective-permute-done), channel_id=1, source_target_pairs={{0,2},{1,3},{2,0},{3,1},{4,6},{5,7},{6,4},{7,5},{8,10},{9,11},{10,... | collective-permute-start | bytes 1572872 | tf_op jit(solution)/shard_map/ppermute | solution.py:121
  51.2 10.4 %collective-permute-done.8 = bf16[256,1024]{1,0:T(8,128)(2,1)} collective-permute-done((bf16[256,1024]{1,0:T(8,128)(2,1)S(1)}, bf16[256,1024]{1,0:T(8,128)(2,1)}, u32[]{:S(2)}, u32[]{:S(2)}) %collective-permute-start.8) | collective-permute-done | bytes 524320 | tf_op jit(solution)/shard_map/ppermute | solution.py:121
  62.7 5.8 %collective-permute-done.9 = bf16[256,1024]{1,0:T(8,128)(2,1)} collective-permute-done((bf16[256,1024]{1,0:T(8,128)(2,1)}, bf16[256,1024]{1,0:T(8,128)(2,1)}, u32[]{:S(2)}, u32[]{:S(2)}) %collective-permute-start.9) | collective-permute-done | bytes 524320 | tf_op jit(solution)/shard_map/ppermute | solution.py:121
  69.6 4.3 %collective-permute-start.11 = (bf16[512,1024]{1,0:T(8,128)(2,1)S(1)}, bf16[512,1024]{1,0:T(8,128)(2,1)}, u32[]{:S(2)}, u32[]{:S(2)}) collective-permute-start(bf16[512,1024]{1,0:T(8,128)(2,1)S(1)} %collective-permute-done.4.refs_4_), channel_id=1, source_target_pairs={{0,4},{8,12},{16,20},{24,28},{1,5},{9,13},{17,21},{25,29},{2,6},{1... | collective-permute-start | bytes 3145736 | tf_op jit(solution)/shard_map/ppermute | solution.py:115
  87.7 4.1 %fusion.2.own_ref.refs_1_ = bf16[2048,1024]{1,0:T(8,128)(2,1)} fusion(bf16[2048,1024]{1,0:T(8,128)(2,1)} %param.2, f32[2048]{0:T(1024)S(1)} %add_rsqrt_fusion), kind=kLoop, calls=%fused_computation.4 | loop fusion | flops 8388608 | bytes 8396800 | tf_op jit(solution)/shard_map/convert_element_type | solution.py:20
  91.8 4.2 %collective-permute-done.11.refs_5_ = bf16[512,1024]{1,0:T(8,128)(2,1)} collective-permute-done((bf16[512,1024]{1,0:T(8,128)(2,1)S(1)}, bf16[512,1024]{1,0:T(8,128)(2,1)}, u32[]{:S(2)}, u32[]{:S(2)}) %collective-permute-start.11) | collective-permute-done | bytes 1048608 | tf_op jit(solution)/shard_map/ppermute | solution.py:115
  96.0 2.0 %far.1 = (f32[1,512]{1,0:T(1,128)S(1)}, f32[1,512]{1,0:T(1,128)S(1)}) custom-call(s32[16]{0:T(128)S(1)} %stack.122.bounds_ref, bf16[512,1024]{1,0:T(8,128)(2,1)S(1)} %constant_dynamic-update-slice_fusion.refs_0_, bf16[512,1024]{1,0:T(8,128)(2,1)} %collective-permute-done.7.refs_1_, bf16[512,1024]{1,0:T(8,128)(2,1)S(1)} %constant_dynamic-update-slice_fusion.2.refs_2_, ...), custom_call_target="tpu_custom_call" | custom-call | flops 4294967296 | bytes 6291456 | tf_op jit(solution)/shard_map/far/pallas_call | solution.py:89
  98.0 1.6 %collective-permute-start.13 = (f32[512]{0:T(512)S(1)}, f32[512]{0:T(512)S(1)}, u32[]{:S(2)}, u32[]{:S(2)}) collective-permute-start(f32[512]{0:T(512)S(1)} %bitcast.52), channel_id=1, source_target_pairs={{4,8},{12,16},{20,24},{5,9},{13,17},{21,25},{6,10},{14,18},{22,26}... | collective-permute-start | bytes 6152 | tf_op jit(solution)/shard_map/ppermute | solution.py:115
  99.6 4.7 %near.1 = (f32[1,2048]{1,0:T(1,128)S(1)}, f32[1,512]{1,0:T(1,128)S(1)}, f32[1,512]{1,0:T(1,128)S(1)}, f32[1,512]{1,0:T(1,128)S(1)}) custom-call(s32[12]{0:T(128)S(1)} %stack.110.bounds_ref, bf16[512,1024]{1,0:T(8,128)(2,1)S(1)} %constant_dynamic-update-slice_fusion.refs_0_, bf16[2048,1024]{1,0:T(8,128)(2,1)} %fusion.2.own_ref.refs_1_, ...), custom_call_target="tpu_custom_call" | custom-call | flops 6442450944 | bytes 8388608 | tf_op jit(solution)/shard_map/near/pallas_call | solution.py:89
  104.3 6.4 %collective-permute-start.12 = (f32[512]{0:T(512)S(1)}, f32[512]{0:T(512)S(1)}, u32[]{:S(2)}, u32[]{:S(2)}) collective-permute-start(f32[512]{0:T(512)S(1)} %bitcast.56), channel_id=1, source_target_pairs={{0,8},{4,12},{8,16},{12,20},{16,24},{20,28},{1,9},{5,13},{9,17},{1... | collective-permute-start | bytes 6152 | tf_op jit(solution)/shard_map/ppermute | solution.py:115
  110.7 12.5 %collective-permute-start.6 = (f32[512]{0:T(512)S(1)}, f32[512]{0:T(512)S(1)}, u32[]{:S(2)}, u32[]{:S(2)}) collective-permute-start(f32[512]{0:T(512)S(1)} %bitcast.53), channel_id=1, source_target_pairs={{0,4},{4,0},{8,12},{12,8},{16,20},{20,16},{24,28},{28,24},{1,5},{5... | collective-permute-start | bytes 6152 | tf_op jit(solution)/shard_map/ppermute | solution.py:118
  123.3 3.2 %diagonal.1 = f32[1,2048]{1,0:T(1,128)S(1)} custom-call(s32[2]{0:T(128)S(1)} %pad_add_fusion.tiles_ref, s32[1,2048]{1,0:T(1,128)S(1)} %bitcast.51, bf16[2048,1024]{1,0:T(8,128)(2,1)S(1)} %copy-done), custom_call_target="tpu_custom_call" | custom-call | flops 1073741824 | bytes 4194304 | tf_op jit(solution)/shard_map/diagonal/pallas_call | solution.py:160
  127.3 6.4 %pmax.7 = f32[2048]{0:T(1024)} all-reduce(f32[2048]{0:T(1024)S(1)} %maximum_maximum_fusion), channel_id=1, replica_groups=mesh['shard'=8,'rep'=4] {'rep'}, use_global_device_ids=true, to_apply=%region_7.8 | all-reduce | flops 2048 | bytes 16384 | tf_op jit(solution)/shard_map/pmax | solution.py:225
  (55 shorter events, 9.4 us)
Async XLA Ops:
  5.5 15.6 %copy-start.1 = (s32[2048]{0:T(1024)S(1)}, s32[2048]{0:T(1024)}, u32[]{:S(2)}) copy-start(s32[2048]{0:T(1024)} %param.3) | copy-start | bytes 24580
  5.5 16.2 %copy-start.2 = (u32[32]{0:T(128)S(1)}, u32[32]{0:T(128)}, u32[]{:S(2)}) copy-start(u32[32]{0:T(128)} %constant.80) | copy-start | bytes 388
  5.5 64.1 %collective-permute-start.4 = (bf16[512,1024]{1,0:T(8,128)(2,1)}, bf16[512,1024]{1,0:T(8,128)(2,1)S(1)}, u32[]{:S(2)}, u32[]{:S(2)}) collective-permute-start(bf16[512,1024]{1,0:T(8,128)(2,1)} %get-tuple-element.22), channel_id=1, source_target_pairs={{8,0},{12,4},{16,8},{20,12},{24,16},{28,20},{9,1},{13,5},{17,9},{2... | collective-permute-start | bytes 3145736 | tf_op jit(solution)/shard_map/ppermute | solution.py:115
  8.8 37.8 %collective-permute-start = (bf16[256,1024]{1,0:T(8,128)(2,1)S(1)}, bf16[256,1024]{1,0:T(8,128)(2,1)S(1)}, u32[]{:S(2)}, u32[]{:S(2)}) collective-permute-start(bf16[256,1024]{1,0:T(8,128)(2,1)S(1)} %get-tuple-element.24), channel_id=1, source_target_pairs={{0,8},{4,12},{8,16},{12,20},{16,24},{20,28},{1,9},{5,13},{9,17},{1... | collective-permute-start | bytes 1572872 | tf_op jit(solution)/shard_map/ppermute | solution.py:115
  12.8 36.0 %collective-permute-start.1 = (bf16[256,1024]{1,0:T(8,128)(2,1)S(1)}, bf16[256,1024]{1,0:T(8,128)(2,1)}, u32[]{:S(2)}, u32[]{:S(2)}) collective-permute-start(bf16[256,1024]{1,0:T(8,128)(2,1)S(1)} %get-tuple-element.23), channel_id=1, source_target_pairs={{0,8},{4,12},{8,16},{12,20},{16,24},{20,28},{1,9},{5,13},{9,17},{1... | collective-permute-start | bytes 1572872 | tf_op jit(solution)/shard_map/ppermute | solution.py:115
  16.3 71.2 %collective-permute-start.2 = (bf16[512,1024]{1,0:T(8,128)(2,1)}, bf16[512,1024]{1,0:T(8,128)(2,1)}, u32[]{:S(2)}, u32[]{:S(2)}) collective-permute-start(bf16[512,1024]{1,0:T(8,128)(2,1)} %get-tuple-element.21), channel_id=1, source_target_pairs={{0,4},{4,0},{8,12},{12,8},{16,20},{20,16},{24,28},{28,24},{1,5},{5... | collective-permute-start | bytes 3145736 | tf_op jit(solution)/shard_map/ppermute | solution.py:118
  46.6 15.0 %collective-permute-start.8 = (bf16[256,1024]{1,0:T(8,128)(2,1)S(1)}, bf16[256,1024]{1,0:T(8,128)(2,1)}, u32[]{:S(2)}, u32[]{:S(2)}) collective-permute-start(bf16[256,1024]{1,0:T(8,128)(2,1)S(1)} %collective-permute-done), channel_id=1, source_target_pairs={{0,2},{1,3},{2,0},{3,1},{4,6},{5,7},{6,4},{7,5},{8,10},{9,11},{10,... | collective-permute-start | bytes 1572872 | tf_op jit(solution)/shard_map/ppermute | solution.py:121
  48.8 19.7 %collective-permute-start.9 = (bf16[256,1024]{1,0:T(8,128)(2,1)}, bf16[256,1024]{1,0:T(8,128)(2,1)}, u32[]{:S(2)}, u32[]{:S(2)}) collective-permute-start(bf16[256,1024]{1,0:T(8,128)(2,1)} %collective-permute-done.1), channel_id=1, source_target_pairs={{0,2},{1,3},{2,0},{3,1},{4,6},{5,7},{6,4},{7,5},{8,10},{9,11},{10,... | collective-permute-start | bytes 1572872 | tf_op jit(solution)/shard_map/ppermute | solution.py:121
  51.1 40.7 %collective-permute-start.7 = (bf16[512,1024]{1,0:T(8,128)(2,1)S(1)}, bf16[512,1024]{1,0:T(8,128)(2,1)}, u32[]{:S(2)}, u32[]{:S(2)}) collective-permute-start(bf16[512,1024]{1,0:T(8,128)(2,1)S(1)} %constant_dynamic-update-slice_fusion.refs_0_), channel_id=1, source_target_pairs={{0,1},{1,0},{2,3},{3,2},{4,5},{5,4},{6,7},{7,6},{8,9},{9,8},{10,11... | collective-permute-start | bytes 3145736 | tf_op jit(solution)/shard_map/ppermute | solution.py:121
  69.5 22.3 %collective-permute-start.10 = (bf16[512,1024]{1,0:T(8,128)(2,1)S(1)}, bf16[512,1024]{1,0:T(8,128)(2,1)}, u32[]{:S(2)}, u32[]{:S(2)}) collective-permute-start(bf16[512,1024]{1,0:T(8,128)(2,1)S(1)} %constant_dynamic-update-slice_fusion.2.refs_2_), channel_id=1, source_target_pairs={{0,1},{1,0},{2,3},{3,2},{4,5},{5,4},{6,7},{7,6},{8,9},{9,8},{10,11... | collective-permute-start | bytes 3145736 | tf_op jit(solution)/shard_map/ppermute | solution.py:121
  69.6 26.4 %collective-permute-start.11 = (bf16[512,1024]{1,0:T(8,128)(2,1)S(1)}, bf16[512,1024]{1,0:T(8,128)(2,1)}, u32[]{:S(2)}, u32[]{:S(2)}) collective-permute-start(bf16[512,1024]{1,0:T(8,128)(2,1)S(1)} %collective-permute-done.4.refs_4_), channel_id=1, source_target_pairs={{0,4},{8,12},{16,20},{24,28},{1,5},{9,13},{17,21},{25,29},{2,6},{1... | collective-permute-start | bytes 3145736 | tf_op jit(solution)/shard_map/ppermute | solution.py:115
  87.5 12.1 %collective-permute-start.3 = (bf16[512,1024]{1,0:T(8,128)(2,1)}, bf16[512,1024]{1,0:T(8,128)(2,1)S(1)}, u32[]{:S(2)}, u32[]{:S(2)}) collective-permute-start(bf16[512,1024]{1,0:T(8,128)(2,1)} %collective-permute-done.2.refs_2_), channel_id=1, source_target_pairs={{0,1},{1,0},{2,3},{3,2},{4,5},{5,4},{6,7},{7,6},{8,9},{9,8},{10,11... | collective-permute-start | bytes 3145736 | tf_op jit(solution)/shard_map/ppermute | solution.py:121
  98.0 25.3 %copy-start = (bf16[2048,1024]{1,0:T(8,128)(2,1)S(1)}, bf16[2048,1024]{1,0:T(8,128)(2,1)}, u32[]{:S(2)}) copy-start(bf16[2048,1024]{1,0:T(8,128)(2,1)} %fusion.2.own_ref.refs_1_) | copy-start | bytes 12582916
  98.0 29.2 %collective-permute-start.13 = (f32[512]{0:T(512)S(1)}, f32[512]{0:T(512)S(1)}, u32[]{:S(2)}, u32[]{:S(2)}) collective-permute-start(f32[512]{0:T(512)S(1)} %bitcast.52), channel_id=1, source_target_pairs={{4,8},{12,16},{20,24},{5,9},{13,17},{21,25},{6,10},{14,18},{22,26}... | collective-permute-start | bytes 6152 | tf_op jit(solution)/shard_map/ppermute | solution.py:115
  104.3 22.9 %collective-permute-start.12 = (f32[512]{0:T(512)S(1)}, f32[512]{0:T(512)S(1)}, u32[]{:S(2)}, u32[]{:S(2)}) collective-permute-start(f32[512]{0:T(512)S(1)} %bitcast.56), channel_id=1, source_target_pairs={{0,8},{4,12},{8,16},{12,20},{16,24},{20,28},{1,9},{5,13},{9,17},{1... | collective-permute-start | bytes 6152 | tf_op jit(solution)/shard_map/ppermute | solution.py:115
  110.7 16.3 %collective-permute-start.6 = (f32[512]{0:T(512)S(1)}, f32[512]{0:T(512)S(1)}, u32[]{:S(2)}, u32[]{:S(2)}) collective-permute-start(f32[512]{0:T(512)S(1)} %bitcast.53), channel_id=1, source_target_pairs={{0,4},{4,0},{8,12},{12,8},{16,20},{20,16},{24,28},{28,24},{1,5},{5... | collective-permute-start | bytes 6152 | tf_op jit(solution)/shard_map/ppermute | solution.py:118
  123.2 3.6 %collective-permute-start.5 = (f32[512]{0:T(512)S(1)}, f32[512]{0:T(512)S(1)}, u32[]{:S(2)}, u32[]{:S(2)}) collective-permute-start(f32[512]{0:T(512)S(1)} %bitcast.54), channel_id=1, source_target_pairs={{0,4},{4,0},{8,12},{12,8},{16,20},{20,16},{24,28},{28,24},{1,5},{5... | collective-permute-start | bytes 6152 | tf_op jit(solution)/shard_map/ppermute | solution.py:118

commit v2 on v0

v2 whole, which is shorter than its diff:
```python
import functools
import math

import jax
import jax.numpy as jnp
from jax import lax
from jax.experimental import pallas as pl
from jax.experimental.pallas import tpu as pltpu
from jax.sharding import PartitionSpec as P

F32 = jnp.float32
BF16 = jnp.bfloat16
TILE = 256
WIDE = 512
INFO = 16
VMEM_LIMIT = 48 * 1024 * 1024
VMEM = pl.BlockSpec(memory_space=pltpu.VMEM)
SMEM = pl.BlockSpec(memory_space=pltpu.SMEM)


def normalize(values):
    as_float = values.astype(F32)
    inverse = lax.rsqrt(jnp.mean(as_float * as_float, axis=1, keepdims=True) + 1e-06)
    return (as_float * inverse / math.sqrt(values.shape[1])).astype(BF16)


def score(keys, queries):
    return lax.dot_general(keys, queries, (((1,), (1,)), ((), ())), preferred_element_type=F32)


def fold(values):
    rows, cols = values.shape
    return jnp.max(values.reshape(rows // 8, 8, cols), axis=0)


def prepare_kernel(index_ref, mine_ref, across_ref, labels_ref, a_out, b_out, mine_out, across_out):
    labels = labels_ref[...]
    first, last = jnp.min(labels), jnp.max(labels)
    head = jnp.sum((labels == first).astype(jnp.int32))
    tail = jnp.sum((labels == last).astype(jnp.int32))
    row = lax.broadcasted_iota(jnp.int32, (INFO, mine_ref.shape[1]), 0)
    info = jnp.zeros(row.shape, jnp.int32)
    for n, value in enumerate([first, last, head // 16, head % 16, tail // 16, tail % 16]):
        info = jnp.where(row == n, value, info)
    info = info.astype(F32).astype(BF16)
    rows = mine_ref.shape[0]
    half = rows // 2
    for n in range(rows // 128):
        part = normalize(mine_ref[pl.ds(n * 128, 128), :])
        mine_out[pl.ds(n * 128, 128), :] = part
        if n * 128 < half:
            a_out[pl.ds(n * 128, 128), :] = part
        else:
            b_out[pl.ds(n * 128 - half, 128), :] = part
        across_out[pl.ds(n * 128, 128), :] = normalize(across_ref[pl.ds(n * 128, 128), :])
    b_out[pl.ds(half, INFO), :] = info
    mine_out[pl.ds(rows, INFO), :] = info
    across_out[pl.ds(rows, INFO), :] = info


def read_info(ref):
    block = ref[pl.ds(ref.shape[0] - INFO, INFO), pl.ds(0, 128)].astype(F32)

    def scalar(values):
        return jnp.max(values).astype(jnp.int32)

    return (
        scalar(block[0:1]),
        scalar(block[1:2]),
        scalar(block[2:3] * 16 + block[3:4]),
        scalar(block[4:5] * 16 + block[5:6]),
    )


def rectangle(keys_ref, key_rows, queries_ref, query_rows, out_ref, out_at, first_key, count):
    step = min(WIDE, query_rows)
    count = jnp.where(first_key < key_rows, count, 0)

    def over_queries(j, _):
        at = pl.multiple_of(j * step, step)
        queries = queries_ref[pl.ds(at, step), :]

        scores = score(keys_ref[pl.ds(0, key_rows), :], queries)
        row = lax.broadcasted_iota(jnp.int32, scores.shape, 0)
        best = fold(jnp.where(row >= first_key, scores, -1.0))
        best = jnp.max(best, axis=0, keepdims=True)
        col = lax.broadcasted_iota(jnp.int32, best.shape, 1) + at
        cols = pl.ds(pl.multiple_of(out_at + at, TILE), step)
        out_ref[:, cols] = jnp.maximum(out_ref[:, cols], jnp.where(col < count, best, -1.0))
        return 0

    lax.fori_loop(0, (count + step - 1) // step, over_queries, 0)


def own_kernel(place_ref, emb_ref, labels_ref, row_labels_ref, own_out, best_out):
    rows = emb_ref.shape[0]
    for n in range(rows // 128):
        own_out[pl.ds(n * 128, 128), :] = normalize(emb_ref[pl.ds(n * 128, 128), :])
    best_out[...] = jnp.full(best_out.shape, -1.0, F32)
    reps = place_ref[2]
    for n in range(2):
        tile = place_ref[0] if n == 0 else rows // TILE - 1 - place_ref[0]
        at = pl.multiple_of(tile * TILE, TILE)
        keys = own_out[pl.ds(at, TILE), :]
        row_labels = row_labels_ref[pl.ds(at, TILE), :]

        def over_queries(j, _):
            cols = pl.ds(pl.multiple_of(j * WIDE, WIDE), WIDE)
            scores = score(keys, own_out[cols, :])
            row = lax.broadcasted_iota(jnp.int32, scores.shape, 0) + at
            col = lax.broadcasted_iota(jnp.int32, scores.shape, 1) + j * WIDE
            keep = (row_labels == labels_ref[:, cols]) & (row < col)
            best = jnp.max(fold(jnp.where(keep, scores, -1.0)), axis=0, keepdims=True)
            best_out[:, cols] = jnp.maximum(best_out[:, cols], best)
            return 0

        lax.fori_loop(at // WIDE, rows // WIDE, over_queries, 0)


def near_kernel(
    place_ref, own_ref, mine_ref, best_ref, low_a, low_b, low_1a, low_1b, part_a, part_b, high,
    best_out, part_out, high_out,
):
    rows = own_ref.shape[0]
    quarter = part_a.shape[0] - INFO
    half = quarter // 2
    rep, odd, _, part = [place_ref[n] for n in range(4)]
    mine, low, other, up = [read_info(ref) for ref in (mine_ref, low_b, part_a, high)]
    best_out[...] = best_ref[...]
    part_out[...] = jnp.full(part_out.shape, -1.0, F32)
    high_out[...] = jnp.full(high_out.shape, -1.0, F32)

    def reach(query, key, offset, limit):
        count = jnp.clip(query[2] - offset, 0, limit)
        return jnp.where(query[0] == key[1], count, 0)

    def first(key, at, limit):
        return jnp.clip(rows - key[3] - at, 0, limit)

    lows = [(low_a, rep * quarter), (low_b, rep * quarter + half)]
    lows_1 = [(low_1a, (rep ^ 1) * quarter), (low_1b, (rep ^ 1) * quarter + half)]
    for keys, at in lows:
        rectangle(keys, half, own_ref, rows, best_out, 0, first(low, at, half), reach(mine, low, 0, rows))
    count = jnp.where(odd == 1, reach(mine, other, 0, rows), 0)
    rectangle(part_a, quarter, own_ref, rows, best_out, 0, first(other, part * quarter, quarter), count)
    for n, queries in enumerate([part_a, part_b]):
        index = part ^ n
        for keys, at in lows:
            rectangle(
                keys, half, queries, quarter, part_out, n * quarter,
                first(low, at, half), reach(other, low, index * quarter, quarter),
            )
        rectangle(
            queries, quarter, high, quarter, high_out, 0,
            first(other, index * quarter, quarter), reach(up, other, rep * quarter, quarter),
        )
    for keys, at in lows + lows_1:
        rectangle(
            keys, half, high, quarter, high_out, 0,
            first(low, at, half), reach(up, low, rep * quarter, quarter),
        )


def far_kernel(
    place_ref, prior_ref, low_a, low_b, low_1a, low_1b, low_2a, low_2b, low_3a, low_3b,
    high, up_a, up_b, high_out, up_out,
):
    rows = place_ref[4]
    quarter = high.shape[0] - INFO
    half = quarter // 2
    rep = place_ref[0]
    low, up, side = [read_info(ref) for ref in (low_b, high, up_b)]
    high_out[...] = prior_ref[...]
    up_out[...] = jnp.full(up_out.shape, -1.0, F32)

    def reach(query, offset, limit):
        count = jnp.clip(query[2] - offset, 0, limit)
        return jnp.where(query[0] == low[1], count, 0)

    pieces = [(low_a, low_b), (low_1a, low_1b), (low_2a, low_2b), (low_3a, low_3b)]
    for n, pair in enumerate(pieces):
        for m, keys in enumerate(pair):
            at = (rep ^ n) * quarter + m * half
            first = jnp.clip(rows - low[3] - at, 0, half)
            if n >= 2:
                rectangle(keys, half, high, quarter, high_out, 0, first, reach(up, rep * quarter, quarter))
            rectangle(keys, half, up_a, half, up_out, 0, first, reach(side, (rep ^ 2) * quarter, half))
            rectangle(
                keys, half, up_b, half, up_out, half, first, reach(side, rep * quarter + half, half)
            )


def local(embeddings, labels):
    rows, width = embeddings.shape
    shards, reps = lax.axis_size("shard"), lax.axis_size("rep")
    s, r = lax.axis_index("shard"), lax.axis_index("rep")
    odd = s % 2
    quarter = rows // reps
    half = quarter // 2

    def along_shard(block, distance, keep=lambda i: True):
        route = [
            (i, i + distance) for i in range(shards) if i + distance in range(shards) and keep(i)
        ]
        return lax.ppermute(block, "shard", route)

    def partner(block):
        return lax.ppermute(block, "shard", [(i, i ^ 1) for i in range(shards)])

    def other_rep(block, flip):
        return lax.ppermute(block, "rep", [(i, i ^ flip) for i in range(reps)])

    def call(kernel, name, shapes, work, in_specs, *arrays):
        return pl.pallas_call(
            kernel,
            out_shape=[jax.ShapeDtypeStruct(shape, dtype) for shape, dtype in shapes],
            in_specs=in_specs,
            out_specs=[VMEM] * len(shapes),
            compiler_params=pltpu.CompilerParams(vmem_limit_bytes=VMEM_LIMIT),
            cost_estimate=pl.CostEstimate(
                flops=int(2 * work * rows * rows * width),
                bytes_accessed=sum(a.size * a.dtype.itemsize for a in arrays),
                transcendentals=0,
            ),
            name=name,
        )(*arrays)

    sent = jnp.where(odd == 1, r, r ^ 2)
    part = jnp.where(odd == 1, r ^ 2, r)
    place = jnp.stack([r, odd, jnp.int32(reps), part, jnp.int32(rows)]).astype(jnp.int32)
    piece_shape = jax.ShapeDtypeStruct((quarter + INFO, width), BF16)
    piece_spec = pl.BlockSpec((quarter + INFO, width), lambda i, at: (0, 0))
    half_spec = pl.BlockSpec((half, width), lambda i, at: (0, 0))
    tail_spec = pl.BlockSpec((half + INFO, width), lambda i, at: (0, 0))
    mine_a, mine_b, mine, across_mine = pl.pallas_call(
        prepare_kernel,
        out_shape=[
            jax.ShapeDtypeStruct((half, width), BF16),
            jax.ShapeDtypeStruct((half + INFO, width), BF16),
            piece_shape,
            piece_shape,
        ],
        grid_spec=pltpu.PrefetchScalarGridSpec(
            num_scalar_prefetch=1,
            grid=(1,),
            in_specs=[
                pl.BlockSpec((quarter, width), lambda i, at: (at[0], 0)),
                pl.BlockSpec((quarter, width), lambda i, at: (at[1], 0)),
                pl.BlockSpec((rows // 128, 128), lambda i, at: (0, 0)),
            ],
            out_specs=[half_spec, tail_spec, piece_spec, piece_spec],
        ),
        compiler_params=pltpu.CompilerParams(vmem_limit_bytes=VMEM_LIMIT),
        name="prepare",
    )(jnp.stack([r, sent]).astype(jnp.int32), embeddings, embeddings, labels.reshape(rows // 128, 128))

    low_a = along_shard(mine_a, 2)
    high = along_shard(mine, -2)
    across = partner(across_mine)
    low_b = along_shard(mine_b, 2)

    own, best = call(
        own_kernel, "own", [((rows, width), BF16), ((1, rows), F32)], 0.15,
        [SMEM, VMEM, VMEM, VMEM], place, embeddings, labels[None, :], labels[:, None],
    )

    odd_only, even_only = (lambda i: i % 2 == 1), (lambda i: i % 2 == 0)
    low_2a = other_rep(low_a, 2)
    low_1a = other_rep(low_a, 1)
    low_2b = other_rep(low_b, 2)
    up_b = along_shard(high[half:], 1, even_only)
    up_a = along_shard(across[:half], -2, odd_only)
    across_1 = other_rep(across, 1)
    low_1b = other_rep(low_b, 1)
    low_3a = other_rep(low_2a, 1)
    low_3b = other_rep(low_2b, 1)

    best, of_part, of_high = call(
        near_kernel, "near",
        [((1, rows), F32), ((1, 2 * quarter), F32), ((1, quarter), F32)], 0.75,
        [SMEM] + [VMEM] * 10,
        place, own, mine, best, low_a, low_b, low_1a, low_1b, across, across_1, high,
    )
    from_partner = partner(of_part)

    of_high, of_up = call(
        far_kernel, "far", [((1, quarter), F32), ((1, quarter), F32)], 0.4,
        [SMEM] + [VMEM] * 12,
        place, of_high, low_a, low_b, low_1a, low_1b, low_2a, low_2b, low_3a, low_3b,
        high, up_a, up_b,
    )

    above = jnp.where(s >= 2, along_shard(of_high, 2)[0], -1.0)
    beside = jnp.where((s >= 2) & (odd == 0), along_shard(of_up, 1, odd_only)[0], -1.0)

    def placed(values, at):
        return lax.dynamic_update_slice_in_dim(jnp.full((rows,), -1.0, F32), values, at, 0)

    home = jnp.where(odd == 1, r, r ^ 2)
    best = jnp.maximum(best[0], placed(from_partner[0, :quarter], home * quarter))
    best = jnp.maximum(best, placed(from_partner[0, quarter:], (home ^ 1) * quarter))
    best = jnp.maximum(best, placed(above, r * quarter))
    best = jnp.maximum(best, placed(beside[:half], (r ^ 2) * quarter))
    best = jnp.maximum(best, placed(beside[half:], r * quarter + half))
    return lax.pmax(best, "rep")


def solution(mesh):
    placed = (P("shard", None), P("shard"))
    return jax.shard_map(local, mesh=mesh, in_specs=placed, out_specs=P("shard"), check_vma=False)
```

time: 170 us -> 95.1 us (0.56)
  the two profiles are of different devices: /device:TPU:18 before, /device:TPU:8 now
where the time goes in v2:
time: 95.1 us; the launch traced here: 95.2 us
  starting transfers between devices  33 us (35%)
  waiting for transfers between devices  32.6 us (34%)
  Pallas kernels  17.4 us (18%)
  blocking collectives  6.44 us (7%)
  local copies, waits for them, and re-layouts  5.37 us (6%)
    ppermute x7, starting transfers between devices, along_shard(): return lax.ppermute(block, 'shard', route)  21 us
    ppermute x2, waiting for transfers between devices, partner(): return lax.ppermute(block, 'shard', [(i, i ^ 1) for i in range(shards)])  14.7 us
    pallas_call x3, Pallas kernels, call(): pl.pallas_call(kernel, out_shape=[jax.ShapeDtypeStruct(shape, dtype) for...  14.5 us
    ppermute x7, waiting for transfers between devices, other_rep(): return lax.ppermute(block, 'rep', [(i, i ^ flip) for i in range(reps)])  10.3 us
    ppermute x2, starting transfers between devices, partner(): return lax.ppermute(block, 'shard', [(i, i ^ 1) for i in range(shards)])  8.43 us
    ppermute x7, waiting for transfers between devices, along_shard(): return lax.ppermute(block, 'shard', route)  7.64 us
    pmax x1, blocking collectives, local(): return lax.pmax(best, 'rep')  6.44 us
    ppermute x7, starting transfers between devices, other_rep(): return lax.ppermute(block, 'rep', [(i, i ^ flip) for i in range(reps)])  3.64 us
  transfers between devices with their start and end apart: 16, of which 5 were waited for; matrix products, arithmetic and copies ran while one was open for 2% of the time, Pallas kernels for 12%

profile of v2, /device:TPU:8, one launch (start us, length us, event | category | flops | bytes accessed | tf_op | source)
XLA Modules:
  0.0 95.2 jit_solution(11885823777978192941)
XLA Ops:
  0.1 0.7 copy-done
  0.8 2.9 %prepare.1 = (bf16[256,1024]{1,0:T(8,128)(2,1)S(1)}, bf16[272,1024]{1,0:T(8,128)(2,1)S(1)}, bf16[528,1024]{1,0:T(8,128)(2,1)S(1)}, bf16[528,1024]{1,0:T(8,128)(2,1)S(1)}) custom-call(s32[2]{0:T(128)S(1)} %pad_add_fusion.index_ref, bf16[2048,1024]{1,0:T(8,128)(2,1)} %across_ref.1, bf16[2048,1024]{1,0:T(8,128)(2,1)} %across_ref.1, s32[16,128]{1,0:T(8,128)S(1)} %bitcast.13), custom_call_target="tpu_custom_call" | custom-call | tf_op jit(solution)/shard_map/prepare/pallas_call | solution.py:235
  3.7 1.6 %collective-permute-start.4 = (bf16[528,1024]{1,0:T(8,128)(2,1)S(1)}, bf16[528,1024]{1,0:T(8,128)(2,1)S(1)}, u32[]{:S(2)}, u32[]{:S(2)}) collective-permute-start(bf16[528,1024]{1,0:T(8,128)(2,1)S(1)} %get-tuple-element.21), channel_id=1, source_target_pairs={{0,4},{4,0},{8,12},{12,8},{16,20},{20,16},{24,28},{28,24},{1,5},{5... | collective-permute-start | bytes 3244040 | tf_op jit(solution)/shard_map/ppermute | solution.py:208
  5.3 3.5 %collective-permute-start = (bf16[256,1024]{1,0:T(8,128)(2,1)S(1)}, bf16[256,1024]{1,0:T(8,128)(2,1)}, u32[]{:S(2)}, u32[]{:S(2)}) collective-permute-start(bf16[256,1024]{1,0:T(8,128)(2,1)S(1)} %get-tuple-element.19), channel_id=1, source_target_pairs={{0,8},{4,12},{8,16},{12,20},{16,24},{20,28},{1,9},{5,13},{9,17},{1... | collective-permute-start | bytes 1572872 | tf_op jit(solution)/shard_map/ppermute | solution.py:205
  8.8 3.5 %collective-permute-start.1 = (bf16[272,1024]{1,0:T(8,128)(2,1)S(1)}, bf16[272,1024]{1,0:T(8,128)(2,1)}, u32[]{:S(2)}, u32[]{:S(2)}) collective-permute-start(bf16[272,1024]{1,0:T(8,128)(2,1)S(1)} %get-tuple-element.20), channel_id=1, source_target_pairs={{0,8},{4,12},{8,16},{12,20},{16,24},{20,28},{1,9},{5,13},{9,17},{1... | collective-permute-start | bytes 1671176 | tf_op jit(solution)/shard_map/ppermute | solution.py:205
  12.3 3.2 %collective-permute-start.6 = (bf16[528,1024]{1,0:T(8,128)(2,1)S(1)}, bf16[528,1024]{1,0:T(8,128)(2,1)}, u32[]{:S(2)}, u32[]{:S(2)}) collective-permute-start(bf16[528,1024]{1,0:T(8,128)(2,1)S(1)} %get-tuple-element.17.mine_ref), channel_id=1, source_target_pairs={{8,0},{12,4},{16,8},{20,12},{24,16},{28,20},{9,1},{13,5},{17,9},{2... | collective-permute-start | bytes 3244040 | tf_op jit(solution)/shard_map/ppermute | solution.py:205
  15.5 13.9 %collective-permute-done.4.part_a = bf16[528,1024]{1,0:T(8,128)(2,1)S(1)} collective-permute-done((bf16[528,1024]{1,0:T(8,128)(2,1)S(1)}, bf16[528,1024]{1,0:T(8,128)(2,1)S(1)}, u32[]{:S(2)}, u32[]{:S(2)}) %collective-permute-start.4) | collective-permute-done | bytes 1081376 | tf_op jit(solution)/shard_map/ppermute | solution.py:208
  29.4 1.5 %collective-permute-start.8 = (bf16[256,1024]{1,0:T(8,128)(2,1)}, bf16[256,1024]{1,0:T(8,128)(2,1)}, u32[]{:S(2)}, u32[]{:S(2)}) collective-permute-start(bf16[256,1024]{1,0:T(8,128)(2,1)} %collective-permute-done.low_a), channel_id=1, source_target_pairs={{0,2},{1,3},{2,0},{3,1},{4,6},{5,7},{6,4},{7,5},{8,10},{9,11},{10,... | collective-permute-start | bytes 1572872 | tf_op jit(solution)/shard_map/ppermute | solution.py:211
  30.9 1.7 %collective-permute-done.1.low_b = bf16[272,1024]{1,0:T(8,128)(2,1)} collective-permute-done((bf16[272,1024]{1,0:T(8,128)(2,1)S(1)}, bf16[272,1024]{1,0:T(8,128)(2,1)}, u32[]{:S(2)}, u32[]{:S(2)}) %collective-permute-start.1) | collective-permute-done | bytes 557088 | tf_op jit(solution)/shard_map/ppermute | solution.py:205
  32.6 1.5 %collective-permute-start.9 = (bf16[272,1024]{1,0:T(8,128)(2,1)}, bf16[272,1024]{1,0:T(8,128)(2,1)}, u32[]{:S(2)}, u32[]{:S(2)}) collective-permute-start(bf16[272,1024]{1,0:T(8,128)(2,1)} %collective-permute-done.1.low_b), channel_id=1, source_target_pairs={{0,2},{1,3},{2,0},{3,1},{4,6},{5,7},{6,4},{7,5},{8,10},{9,11},{10,... | collective-permute-start | bytes 1671176 | tf_op jit(solution)/shard_map/ppermute | solution.py:211
  34.1 10.3 %collective-permute-done.8.low_2a = bf16[256,1024]{1,0:T(8,128)(2,1)} collective-permute-done((bf16[256,1024]{1,0:T(8,128)(2,1)}, bf16[256,1024]{1,0:T(8,128)(2,1)}, u32[]{:S(2)}, u32[]{:S(2)}) %collective-permute-start.8) | collective-permute-done | bytes 524320 | tf_op jit(solution)/shard_map/ppermute | solution.py:211
  44.9 6.4 %own.1 = (bf16[2048,1024]{1,0:T(8,128)(2,1)S(1)}, f32[1,2048]{1,0:T(1,128)S(1)}) custom-call(s32[5]{0:T(128)S(1)} %stack.22.place_ref, bf16[2048,1024]{1,0:T(8,128)(2,1)} %across_ref.1, s32[1,2048]{1,0:T(1,128)S(1)} %bitcast.15, s32[2048,1]{1,0:T(8,128)S(1)} %copy.3.row_labels_ref), custom_call_target="tpu_custom_call" | custom-call | flops 1288490240 | bytes 4210708 | tf_op jit(solution)/shard_map/own/pallas_call | solution.py:214
  51.3 1.9 %copy-done.2 = bf16[2048,1024]{1,0:T(8,128)(2,1)} copy-done((bf16[2048,1024]{1,0:T(8,128)(2,1)}, bf16[2048,1024]{1,0:T(8,128)(2,1)S(1)}, u32[]{:S(2)}) %copy-start.2) | copy-done | bytes 4194328
  53.8 1.1 %slice.35 = bf16[272,1024]{1,0:T(8,128)(2,1)S(1)} slice(bf16[528,1024]{1,0:T(8,128)(2,1)} %collective-permute-done.6.high), slice={[256:528], [0:1024]} | slice | bytes 1114112 | tf_op jit(solution)/shard_map/slice | solution.py:271
  54.9 3.5 %collective-permute-start.13 = (bf16[272,1024]{1,0:T(8,128)(2,1)S(1)}, bf16[272,1024]{1,0:T(8,128)(2,1)S(1)}, u32[]{:S(2)}, u32[]{:S(2)}) collective-permute-start(bf16[272,1024]{1,0:T(8,128)(2,1)S(1)} %slice.35), channel_id=1, source_target_pairs={{0,4},{8,12},{16,20},{24,28},{1,5},{9,13},{17,21},{25,29},{2,6},{1... | collective-permute-start | bytes 1671176 | tf_op jit(solution)/shard_map/ppermute | solution.py:205
  58.4 0.7 collective-permute-start.12
  59.2 5.3 %near.1 = (f32[1,2048]{1,0:T(1,128)S(1)}, f32[1,1024]{1,0:T(1,128)S(1)}, f32[1,512]{1,0:T(1,128)S(1)}) custom-call(s32[5]{0:T(128)S(1)} %stack.22.place_ref, bf16[2048,1024]{1,0:T(8,128)(2,1)} %copy-done.2, bf16[528,1024]{1,0:T(8,128)(2,1)S(1)} %get-tuple-element.17.mine_ref, f32[1,2048]{1,0:T(1,128)S(1)} %get-tuple-element.18.best_ref, ...), custom_call_target="tpu_custom_call" | custom-call | flops 6442450944 | bytes 10690580 | tf_op jit(solution)/shard_map/near/pallas_call | solution.py:214
  64.5 5.9 %collective-permute-done.13.up_b = bf16[272,1024]{1,0:T(8,128)(2,1)S(1)} collective-permute-done((bf16[272,1024]{1,0:T(8,128)(2,1)S(1)}, bf16[272,1024]{1,0:T(8,128)(2,1)S(1)}, u32[]{:S(2)}, u32[]{:S(2)}) %collective-permute-start.13) | collective-permute-done | bytes 557088 | tf_op jit(solution)/shard_map/ppermute | solution.py:205
  70.4 2.8 %far.1 = (f32[1,512]{1,0:T(1,128)S(1)}, f32[1,512]{1,0:T(1,128)S(1)}) custom-call(s32[5]{0:T(128)S(1)} %stack.22.place_ref, f32[1,512]{1,0:T(1,128)S(1)} %get-tuple-element.24.prior_ref, bf16[256,1024]{1,0:T(8,128)(2,1)} %collective-permute-done.low_a, bf16[272,1024]{1,0:T(8,128)(2,1)} %collective-permute-done.1.low_b, ...), custom_call_target="tpu_custom_call" | custom-call | flops 3435973888 | bytes 6490132 | tf_op jit(solution)/shard_map/far/pallas_call | solution.py:214
  73.2 5.4 %collective-permute-start.14 = (f32[1,512]{1,0:T(1,128)S(1)}, f32[1,512]{1,0:T(1,128)S(1)}, u32[]{:S(2)}, u32[]{:S(2)}) collective-permute-start(f32[1,512]{1,0:T(1,128)S(1)} %get-tuple-element.25), channel_id=1, source_target_pairs={{0,8},{4,12},{8,16},{12,20},{16,24},{20,28},{1,9},{5,13},{9,17},{1... | collective-permute-start | bytes 6152 | tf_op jit(solution)/shard_map/ppermute | solution.py:205
  78.7 1.3 %collective-permute-start.15 = (f32[1,512]{1,0:T(1,128)S(1)}, f32[1,512]{1,0:T(1,128)S(1)}, u32[]{:S(2)}, u32[]{:S(2)}) collective-permute-start(f32[1,512]{1,0:T(1,128)S(1)} %get-tuple-element.26), channel_id=1, source_target_pairs={{4,8},{12,16},{20,24},{5,9},{13,17},{21,25},{6,10},{14,18},{22,26}... | collective-permute-start | bytes 6152 | tf_op jit(solution)/shard_map/ppermute | solution.py:205
  80.0 6.8 %collective-permute-start.7 = (f32[1,1024]{1,0:T(1,128)S(1)}, f32[1,1024]{1,0:T(1,128)S(1)}, u32[]{:S(2)}, u32[]{:S(2)}) collective-permute-start(f32[1,1024]{1,0:T(1,128)S(1)} %get-tuple-element.23), channel_id=1, source_target_pairs={{0,4},{4,0},{8,12},{12,8},{16,20},{20,16},{24,28},{28,24},{1,5},{5... | collective-permute-start | bytes 12296 | tf_op jit(solution)/shard_map/ppermute | solution.py:208
  87.6 0.8 collective-permute-done.7
  88.8 6.4 %pmax.7 = f32[2048]{0:T(1024)} all-reduce(f32[2048]{0:T(1024)S(1)} %maximum_maximum_fusion), channel_id=1, replica_groups=mesh['shard'=8,'rep'=4] {'rep'}, use_global_device_ids=true, to_apply=%region_0.1 | all-reduce | flops 2048 | bytes 16384 | tf_op jit(solution)/shard_map/pmax | solution.py:305
  (39 shorter events, 2.4 us)
Async XLA Ops:
  0.1 0.7 copy-start
  0.8 43.6 %copy-start.1 = (s32[2048]{0:T(1024)S(1)}, s32[2048]{0:T(1024)}, u32[]{:S(2)}) copy-start(s32[2048]{0:T(1024)} %param.3) | copy-start | bytes 24580
  3.7 25.7 %collective-permute-start.4 = (bf16[528,1024]{1,0:T(8,128)(2,1)S(1)}, bf16[528,1024]{1,0:T(8,128)(2,1)S(1)}, u32[]{:S(2)}, u32[]{:S(2)}) collective-permute-start(bf16[528,1024]{1,0:T(8,128)(2,1)S(1)} %get-tuple-element.21), channel_id=1, source_target_pairs={{0,4},{4,0},{8,12},{12,8},{16,20},{20,16},{24,28},{28,24},{1,5},{5... | collective-permute-start | bytes 3244040 | tf_op jit(solution)/shard_map/ppermute | solution.py:208
  5.3 24.1 %collective-permute-start = (bf16[256,1024]{1,0:T(8,128)(2,1)S(1)}, bf16[256,1024]{1,0:T(8,128)(2,1)}, u32[]{:S(2)}, u32[]{:S(2)}) collective-permute-start(bf16[256,1024]{1,0:T(8,128)(2,1)S(1)} %get-tuple-element.19), channel_id=1, source_target_pairs={{0,8},{4,12},{8,16},{12,20},{16,24},{20,28},{1,9},{5,13},{9,17},{1... | collective-permute-start | bytes 1572872 | tf_op jit(solution)/shard_map/ppermute | solution.py:205
  8.8 23.8 %collective-permute-start.1 = (bf16[272,1024]{1,0:T(8,128)(2,1)S(1)}, bf16[272,1024]{1,0:T(8,128)(2,1)}, u32[]{:S(2)}, u32[]{:S(2)}) collective-permute-start(bf16[272,1024]{1,0:T(8,128)(2,1)S(1)} %get-tuple-element.20), channel_id=1, source_target_pairs={{0,8},{4,12},{8,16},{12,20},{16,24},{20,28},{1,9},{5,13},{9,17},{1... | collective-permute-start | bytes 1671176 | tf_op jit(solution)/shard_map/ppermute | solution.py:205
  12.3 41.0 %collective-permute-start.6 = (bf16[528,1024]{1,0:T(8,128)(2,1)S(1)}, bf16[528,1024]{1,0:T(8,128)(2,1)}, u32[]{:S(2)}, u32[]{:S(2)}) collective-permute-start(bf16[528,1024]{1,0:T(8,128)(2,1)S(1)} %get-tuple-element.17.mine_ref), channel_id=1, source_target_pairs={{8,0},{12,4},{16,8},{20,12},{24,16},{28,20},{9,1},{13,5},{17,9},{2... | collective-permute-start | bytes 3244040 | tf_op jit(solution)/shard_map/ppermute | solution.py:205
  29.4 29.9 %collective-permute-start.5 = (bf16[528,1024]{1,0:T(8,128)(2,1)S(1)}, bf16[528,1024]{1,0:T(8,128)(2,1)}, u32[]{:S(2)}, u32[]{:S(2)}) collective-permute-start(bf16[528,1024]{1,0:T(8,128)(2,1)S(1)} %collective-permute-done.4.part_a), channel_id=1, source_target_pairs={{0,1},{1,0},{2,3},{3,2},{4,5},{5,4},{6,7},{7,6},{8,9},{9,8},{10,11... | collective-permute-start | bytes 3244040 | tf_op jit(solution)/shard_map/ppermute | solution.py:211
  29.4 15.0 %collective-permute-start.8 = (bf16[256,1024]{1,0:T(8,128)(2,1)}, bf16[256,1024]{1,0:T(8,128)(2,1)}, u32[]{:S(2)}, u32[]{:S(2)}) collective-permute-start(bf16[256,1024]{1,0:T(8,128)(2,1)} %collective-permute-done.low_a), channel_id=1, source_target_pairs={{0,2},{1,3},{2,0},{3,1},{4,6},{5,7},{6,4},{7,5},{8,10},{9,11},{10,... | collective-permute-start | bytes 1572872 | tf_op jit(solution)/shard_map/ppermute | solution.py:211
  32.6 25.8 %collective-permute-start.3 = (bf16[272,1024]{1,0:T(8,128)(2,1)}, bf16[272,1024]{1,0:T(8,128)(2,1)}, u32[]{:S(2)}, u32[]{:S(2)}) collective-permute-start(bf16[272,1024]{1,0:T(8,128)(2,1)} %collective-permute-done.1.low_b), channel_id=1, source_target_pairs={{0,1},{1,0},{2,3},{3,2},{4,5},{5,4},{6,7},{7,6},{8,9},{9,8},{10,11... | collective-permute-start | bytes 1671176 | tf_op jit(solution)/shard_map/ppermute | solution.py:211
  32.6 26.5 %collective-permute-start.9 = (bf16[272,1024]{1,0:T(8,128)(2,1)}, bf16[272,1024]{1,0:T(8,128)(2,1)}, u32[]{:S(2)}, u32[]{:S(2)}) collective-permute-start(bf16[272,1024]{1,0:T(8,128)(2,1)} %collective-permute-done.1.low_b), channel_id=1, source_target_pairs={{0,2},{1,3},{2,0},{3,1},{4,6},{5,7},{6,4},{7,5},{8,10},{9,11},{10,... | collective-permute-start | bytes 1671176 | tf_op jit(solution)/shard_map/ppermute | solution.py:211
  44.4 10.5 %collective-permute-start.2 = (bf16[256,1024]{1,0:T(8,128)(2,1)}, bf16[256,1024]{1,0:T(8,128)(2,1)}, u32[]{:S(2)}, u32[]{:S(2)}) collective-permute-start(bf16[256,1024]{1,0:T(8,128)(2,1)} %collective-permute-done.low_a), channel_id=1, source_target_pairs={{0,1},{1,0},{2,3},{3,2},{4,5},{5,4},{6,7},{7,6},{8,9},{9,8},{10,11... | collective-permute-start | bytes 1572872 | tf_op jit(solution)/shard_map/ppermute | solution.py:211
  51.3 1.9 %copy-start.2 = (bf16[2048,1024]{1,0:T(8,128)(2,1)}, bf16[2048,1024]{1,0:T(8,128)(2,1)S(1)}, u32[]{:S(2)}) copy-start(bf16[2048,1024]{1,0:T(8,128)(2,1)S(1)} %get-tuple-element.16.own_ref) | copy-start | bytes 12582916
  53.3 11.2 %collective-permute-start.10 = (bf16[256,1024]{1,0:T(8,128)(2,1)}, bf16[256,1024]{1,0:T(8,128)(2,1)S(1)}, u32[]{:S(2)}, u32[]{:S(2)}) collective-permute-start(bf16[256,1024]{1,0:T(8,128)(2,1)} %collective-permute-done.8.low_2a), channel_id=1, source_target_pairs={{0,1},{1,0},{2,3},{3,2},{4,5},{5,4},{6,7},{7,6},{8,9},{9,8},{10,11... | collective-permute-start | bytes 1572872 | tf_op jit(solution)/shard_map/ppermute | solution.py:211
  54.9 15.5 %collective-permute-start.13 = (bf16[272,1024]{1,0:T(8,128)(2,1)S(1)}, bf16[272,1024]{1,0:T(8,128)(2,1)S(1)}, u32[]{:S(2)}, u32[]{:S(2)}) collective-permute-start(bf16[272,1024]{1,0:T(8,128)(2,1)S(1)} %slice.35), channel_id=1, source_target_pairs={{0,4},{8,12},{16,20},{24,28},{1,5},{9,13},{17,21},{25,29},{2,6},{1... | collective-permute-start | bytes 1671176 | tf_op jit(solution)/shard_map/ppermute | solution.py:205
  58.4 6.1 %collective-permute-start.12 = (bf16[256,1024]{1,0:T(8,128)(2,1)S(1)}, bf16[256,1024]{1,0:T(8,128)(2,1)S(1)}, u32[]{:S(2)}, u32[]{:S(2)}) collective-permute-start(bf16[256,1024]{1,0:T(8,128)(2,1)S(1)} %slice.34), channel_id=1, source_target_pairs={{12,4},{20,12},{28,20},{13,5},{21,13},{29,21},{14,6},{22,14},{30,2... | collective-permute-start | bytes 1572872 | tf_op jit(solution)/shard_map/ppermute | solution.py:205
  59.1 11.3 %collective-permute-start.11 = (bf16[272,1024]{1,0:T(8,128)(2,1)}, bf16[272,1024]{1,0:T(8,128)(2,1)S(1)}, u32[]{:S(2)}, u32[]{:S(2)}) collective-permute-start(bf16[272,1024]{1,0:T(8,128)(2,1)} %collective-permute-done.9.low_2b), channel_id=1, source_target_pairs={{0,1},{1,0},{2,3},{3,2},{4,5},{5,4},{6,7},{7,6},{8,9},{9,8},{10,11... | collective-permute-start | bytes 1671176 | tf_op jit(solution)/shard_map/ppermute | solution.py:211
  73.2 13.6 %collective-permute-start.14 = (f32[1,512]{1,0:T(1,128)S(1)}, f32[1,512]{1,0:T(1,128)S(1)}, u32[]{:S(2)}, u32[]{:S(2)}) collective-permute-start(f32[1,512]{1,0:T(1,128)S(1)} %get-tuple-element.25), channel_id=1, source_target_pairs={{0,8},{4,12},{8,16},{12,20},{16,24},{20,28},{1,9},{5,13},{9,17},{1... | collective-permute-start | bytes 6152 | tf_op jit(solution)/shard_map/ppermute | solution.py:205
  78.7 8.1 %collective-permute-start.15 = (f32[1,512]{1,0:T(1,128)S(1)}, f32[1,512]{1,0:T(1,128)S(1)}, u32[]{:S(2)}, u32[]{:S(2)}) collective-permute-start(f32[1,512]{1,0:T(1,128)S(1)} %get-tuple-element.26), channel_id=1, source_target_pairs={{4,8},{12,16},{20,24},{5,9},{13,17},{21,25},{6,10},{14,18},{22,26}... | collective-permute-start | bytes 6152 | tf_op jit(solution)/shard_map/ppermute | solution.py:205
  80.0 8.4 %collective-permute-start.7 = (f32[1,1024]{1,0:T(1,128)S(1)}, f32[1,1024]{1,0:T(1,128)S(1)}, u32[]{:S(2)}, u32[]{:S(2)}) collective-permute-start(f32[1,1024]{1,0:T(1,128)S(1)} %get-tuple-element.23), channel_id=1, source_target_pairs={{0,4},{4,0},{8,12},{12,8},{16,20},{20,16},{24,28},{28,24},{1,5},{5... | collective-permute-start | bytes 12296 | tf_op jit(solution)/shard_map/ppermute | solution.py:208

commit v3 on v2

v3 whole, which is shorter than its diff:
```python
import functools
import math

import jax
import jax.numpy as jnp
from jax import lax
from jax.experimental import pallas as pl
from jax.experimental.pallas import tpu as pltpu
from jax.sharding import PartitionSpec as P

F32 = jnp.float32
BF16 = jnp.bfloat16
TILE = 256
WIDE = 512
INFO = 16
VMEM_LIMIT = 48 * 1024 * 1024
VMEM = pl.BlockSpec(memory_space=pltpu.VMEM)
SMEM = pl.BlockSpec(memory_space=pltpu.SMEM)


def normalize(values):
    as_float = values.astype(F32)
    inverse = lax.rsqrt(jnp.mean(as_float * as_float, axis=1, keepdims=True) + 1e-06)
    return (as_float * inverse / math.sqrt(values.shape[1])).astype(BF16)


def score(keys, queries):
    return lax.dot_general(keys, queries, (((1,), (1,)), ((), ())), preferred_element_type=F32)


def fold(values):
    rows, cols = values.shape
    return jnp.max(values.reshape(rows // 8, 8, cols), axis=0)


def prepare_kernel(index_ref, mine_ref, across_ref, labels_ref, lo_out, lo_info, hi_out, hi_info,
                   across_info, across_out):
    labels = labels_ref[...]
    first, last = jnp.min(labels), jnp.max(labels)
    head = jnp.sum((labels == first).astype(jnp.int32))
    tail = jnp.sum((labels == last).astype(jnp.int32))
    row = lax.broadcasted_iota(jnp.int32, (INFO, mine_ref.shape[1]), 0)
    info = jnp.zeros(row.shape, jnp.int32)
    for n, value in enumerate([first, last, head // 16, head % 16, tail // 16, tail % 16]):
        info = jnp.where(row == n, value, info)
    info = info.astype(F32).astype(BF16)
    half = lo_out.shape[0]
    for n in range(half // 128):
        rows, later = pl.ds(n * 128, 128), pl.ds(half + n * 128, 128)
        lo_out[rows, :] = lo_info[rows, :] = normalize(mine_ref[rows, :])
        hi_out[rows, :] = hi_info[rows, :] = normalize(mine_ref[later, :])
        across_info[rows, :] = normalize(across_ref[rows, :])
        across_out[rows, :] = normalize(across_ref[later, :])
    for ref in (lo_info, hi_info, across_info):
        ref[pl.ds(half, INFO), :] = info


def read_info(ref):
    block = ref[pl.ds(ref.shape[0] - INFO, INFO), pl.ds(0, 128)].astype(F32)

    def scalar(values):
        return jnp.max(values).astype(jnp.int32)

    return (
        scalar(block[0:1]),
        scalar(block[1:2]),
        scalar(block[2:3] * 16 + block[3:4]),
        scalar(block[4:5] * 16 + block[5:6]),
    )


def rectangle(keys_ref, key_rows, queries_ref, query_rows, out_ref, out_at, first_key, count):
    step = min(WIDE, query_rows)
    count = jnp.where(first_key < key_rows, count, 0)

    def over_queries(j, _):
        at = pl.multiple_of(j * step, step)
        queries = queries_ref[pl.ds(at, step), :]

        scores = score(keys_ref[pl.ds(0, key_rows), :], queries)
        row = lax.broadcasted_iota(jnp.int32, scores.shape, 0)
        best = fold(jnp.where(row >= first_key, scores, -1.0))
        best = jnp.max(best, axis=0, keepdims=True)
        col = lax.broadcasted_iota(jnp.int32, best.shape, 1) + at
        cols = pl.ds(pl.multiple_of(out_at + at, TILE), step)
        out_ref[:, cols] = jnp.maximum(out_ref[:, cols], jnp.where(col < count, best, -1.0))
        return 0

    lax.fori_loop(0, (count + step - 1) // step, over_queries, 0)


def own_kernel(place_ref, emb_ref, labels_ref, row_labels_ref, own_out, best_out):
    rows = emb_ref.shape[0]
    for n in range(rows // 128):
        own_out[pl.ds(n * 128, 128), :] = normalize(emb_ref[pl.ds(n * 128, 128), :])
    best_out[...] = jnp.full(best_out.shape, -1.0, F32)
    reps = place_ref[2]
    for n in range(2):
        tile = place_ref[0] if n == 0 else rows // TILE - 1 - place_ref[0]
        at = pl.multiple_of(tile * TILE, TILE)
        keys = own_out[pl.ds(at, TILE), :]
        row_labels = row_labels_ref[pl.ds(at, TILE), :]

        def over_queries(j, _):
            cols = pl.ds(pl.multiple_of(j * WIDE, WIDE), WIDE)
            scores = score(keys, own_out[cols, :])
            row = lax.broadcasted_iota(jnp.int32, scores.shape, 0) + at
            col = lax.broadcasted_iota(jnp.int32, scores.shape, 1) + j * WIDE
            keep = (row_labels == labels_ref[:, cols]) & (row < col)
            best = jnp.max(fold(jnp.where(keep, scores, -1.0)), axis=0, keepdims=True)
            best_out[:, cols] = jnp.maximum(best_out[:, cols], best)
            return 0

        lax.fori_loop(at // WIDE, rows // WIDE, over_queries, 0)


def compare_kernel(names, tasks, outs, fresh, rows, place_ref, *refs):
    count = len(names)
    pieces = dict(zip(names, refs[:count]))
    prior, results = refs[count : len(refs) - len(outs)], refs[len(refs) - len(outs) :]
    results = dict(zip(outs, results))
    for name, ref in zip([name for name in outs if name not in fresh], prior):
        results[name][...] = ref[...]
    for name in fresh:
        results[name][...] = jnp.full(results[name].shape, -1.0, F32)
    quarter = rows // 4
    half = quarter // 2
    rep, odd, _, part = [place_ref[n] for n in range(4)]
    info = {name[5:]: read_info(pieces[name]) for name in names if name.startswith("info_")}

    def where(name):
        kind, tail = name.split("_")
        if kind == "own":
            return 0
        at = half if tail[-1] == "b" else 0
        if kind == "low":
            return (rep ^ int(tail[0])) * quarter + at
        index = {"across": part, "high": rep, "up": rep ^ 2 if tail == "a" else rep}[kind]
        return index * quarter + at

    for keys, queries in tasks:
        key_info, query_info = info[keys.split("_")[0]], info[queries.split("_")[0]]
        limit = rows if queries.startswith("own") else half
        reach = jnp.clip(query_info[2] - where(queries), 0, limit)
        reach = jnp.where(query_info[0] == key_info[1], reach, 0)
        if keys.startswith("across") and queries.startswith("own"):
            reach = jnp.where(odd == 1, reach, 0)
        first = jnp.clip(rows - key_info[3] - where(keys), 0, half)
        out = results[queries.split("_")[0]]
        out_at = half if queries.endswith("_b") else 0
        rectangle(pieces[keys], half, pieces[queries], limit, out, out_at, first, reach)


def merge_kernel(place_ref, best_ref, partner_ref, above_ref, beside_ref, out_ref):
    quarter = above_ref.shape[1]
    half = quarter // 2
    rep, shard, home = [place_ref[n] for n in range(3)]
    out_ref[...] = best_ref[...]

    def raised(at, values):
        cols = pl.ds(pl.multiple_of(at, half), values.shape[1])
        out_ref[:, cols] = jnp.maximum(out_ref[:, cols], values)

    raised(home * quarter, partner_ref[...])
    raised(rep * quarter, jnp.where(shard >= 2, above_ref[...], -1.0))
    beside = jnp.where((shard >= 2) & (shard % 2 == 0), beside_ref[...], -1.0)
    raised((rep ^ 2) * quarter, beside[:, :half])
    raised(rep * quarter + half, beside[:, half:])


def local(embeddings, labels):
    rows, width = embeddings.shape
    shards, reps = lax.axis_size("shard"), lax.axis_size("rep")
    s, r = lax.axis_index("shard"), lax.axis_index("rep")
    odd = s % 2
    quarter = rows // reps
    half = quarter // 2

    def along_shard(block, distance, keep=lambda i: True):
        route = [
            (i, i + distance) for i in range(shards) if i + distance in range(shards) and keep(i)
        ]
        return lax.ppermute(block, "shard", route)

    def partner(block):
        return lax.ppermute(block, "shard", [(i, i ^ 1) for i in range(shards)])

    def other_rep(block, flip):
        return lax.ppermute(block, "rep", [(i, i ^ flip) for i in range(reps)])

    def call(kernel, name, shapes, work, in_specs, *arrays):
        return pl.pallas_call(
            kernel,
            out_shape=[jax.ShapeDtypeStruct(shape, dtype) for shape, dtype in shapes],
            in_specs=in_specs,
            out_specs=[VMEM] * len(shapes),
            compiler_params=pltpu.CompilerParams(vmem_limit_bytes=VMEM_LIMIT),
            cost_estimate=pl.CostEstimate(flops=1024, bytes_accessed=1024, transcendentals=0),
            name=name,
        )(*arrays)

    sent = jnp.where(odd == 1, r ^ 1, r ^ 2)
    part = jnp.where(odd == 1, r ^ 2, r ^ 1)
    place = jnp.stack([r, odd, jnp.int32(reps), part]).astype(jnp.int32)
    sizes = [half, half + INFO, half, half + INFO, half + INFO, half]
    lo, lo_info, hi, hi_info, across_info, across_rest = pl.pallas_call(
        prepare_kernel,
        out_shape=[jax.ShapeDtypeStruct((size, width), BF16) for size in sizes],
        grid_spec=pltpu.PrefetchScalarGridSpec(
            num_scalar_prefetch=1,
            grid=(1,),
            in_specs=[
                pl.BlockSpec((quarter, width), lambda i, at: (at[0], 0)),
                pl.BlockSpec((quarter, width), lambda i, at: (at[1], 0)),
                pl.BlockSpec((rows // 128, 128), lambda i, at: (0, 0)),
            ],
            out_specs=[pl.BlockSpec((size, width), lambda i, at: (0, 0)) for size in sizes],
        ),
        compiler_params=pltpu.CompilerParams(vmem_limit_bytes=VMEM_LIMIT),
        name="prepare",
    )(jnp.stack([r, sent]).astype(jnp.int32), embeddings, embeddings, labels.reshape(rows // 128, 128))

    odd_only, even_only = (lambda i: i % 2 == 1), (lambda i: i % 2 == 0)
    fence = lax.optimization_barrier
    piece = {}

    def compare(name, tasks, infos, prior, outs, work):
        names = sorted({n for task in tasks for n in task})
        arrays = [piece[n] for n in names] + [piece[v] for v in infos.values()]
        names = names + ["info_" + k for k in infos]
        ordered = [k for k in outs if k in prior] + [k for k in outs if k not in prior]
        fresh = [k for k in ordered if k not in prior]
        old = [prior[k] for k in ordered if k in prior]
        shapes = [((1, rows if k == "own" else quarter), F32) for k in ordered]
        given = call(
            functools.partial(compare_kernel, names, tasks, ordered, fresh, rows),
            name, shapes, work, [SMEM] + [VMEM] * (len(arrays) + len(old)),
            place, *arrays, *old,
        )
        return dict(zip(ordered, given))

    piece["low_0a"] = along_shard(lo_info, 2)
    piece["across_a"] = partner(across_info)
    piece["high_b"] = along_shard(hi_info, -2)
    piece["low_0b"] = along_shard(hi, 2)
    piece["high_a"] = along_shard(lo, -2)

    names = ["low_0a", "across_a", "high_b"]
    *fenced, across_rest, own_place = fence(tuple(piece[n] for n in names) + (across_rest, place))
    piece.update(zip(names, fenced))
    piece["across_b"] = partner(across_rest)
    piece["low_2a"] = other_rep(piece["low_0a"], 2)
    piece["up_b"] = along_shard(piece["high_b"], 1, even_only)
    piece["low_1a"] = other_rep(piece["low_0a"], 1)
    own, best = call(
        own_kernel, "own", [((rows, width), BF16), ((1, rows), F32)], 0.15,
        [SMEM, VMEM, VMEM, VMEM], own_place, embeddings, labels[None, :], labels[:, None],
    )
    piece["mine"] = lo_info

    piece["own_x"], piece["mine"] = own, lo_info
    infos = {"own": "mine", "low": "low_0a", "across": "across_a", "high": "high_b"}
    result = compare(
        "near",
        [("low_0a", "own_x"), ("across_a", "own_x"), ("low_0a", "across_a"), ("across_a", "high_b"),
         ("low_0a", "high_b"), ("low_1a", "across_a"), ("low_1a", "high_b")],
        infos, {"own": best}, ["own", "across", "high"], 0.35,
    )

    names = ["low_0b", "high_a", "across_b", "low_1a", "low_2a", "across_a"]
    fenced = fence(tuple(piece[n] for n in names) + (result["high"],))
    piece.update(zip(names, fenced))
    result["high"] = fenced[-1]
    piece["low_2b"] = other_rep(piece["low_0b"], 2)
    piece["up_a"] = along_shard(piece["across_a"], -2, odd_only)
    piece["low_1b"] = other_rep(piece["low_0b"], 1)
    piece["low_3a"] = other_rep(piece["low_2a"], 1)
    near = ["low_0a", "low_0b", "low_1a", "low_2a"]
    result = compare(
        "next",
        [("low_0b", "own_x"), ("across_b", "own_x")]
        + [(k, "across_a") for k in ("low_0b", "low_2a")] + [(k, "across_b") for k in near]
        + [("across_a", "high_a"), ("across_b", "high_a"), ("across_b", "high_b")]
        + [(k, "high_a") for k in near] + [(k, "high_b") for k in ("low_0b", "low_2a")],
        infos, result, ["own", "across", "high"], 0.6,
    )
    piece["low_2b"], result["high"] = fence((piece["low_2b"], result["high"]))
    piece["low_3b"] = other_rep(piece["low_2b"], 1)
    last = ["low_1b", "low_2b", "low_3a", "low_3b"]
    best = result["own"]
    result = compare(
        "far",
        [(k, q) for k in last[:2] for q in ("across_a", "across_b")]
        + [(k, q) for k in last for q in ("high_a", "high_b")]
        + [(k, q) for k in near + last for q in ("up_a", "up_b")],
        {"low": "low_0a", "across": "across_a", "high": "high_b", "up": "up_b"},
        result, ["across", "high", "up"], 0.45,
    )

    above = along_shard(result["high"], 2)
    beside = along_shard(result["up"], 1, odd_only)
    from_partner = partner(result["across"])
    place = jnp.stack([r, s, sent]).astype(jnp.int32)
    (best,) = call(
        merge_kernel, "merge", [((1, rows), F32)], 0.0, [SMEM] + [VMEM] * 4,
        place, best, from_partner, above, beside,
    )
    return lax.pmax(best[0], "rep")


def solution(mesh):
    placed = (P("shard", None), P("shard"))
    return jax.shard_map(local, mesh=mesh, in_specs=placed, out_specs=P("shard"), check_vma=False)
```

time: 95.1 us -> 97.1 us (1.021); the launches traced: 95.2 us -> 95.4 us
  waiting for transfers between devices: 32.6 us -> 25.7 us
  Pallas kernels: 17.4 us -> 21.2 us
  starting transfers between devices: 33 us -> 36.8 us
    ppermute x2 -> x3, waiting for transfers between devices: 14.7 us -> 3.44 us  [partner(): return lax.ppermute(block, 'shard', [(i, i ^ 1) for i in range(shards)])]
    ppermute x7 -> x8, waiting for transfers between devices: 7.64 us -> 18.9 us  [along_shard(): return lax.ppermute(block, 'shard', route)]
    ppermute x7 -> x6, waiting for transfers between devices: 10.3 us -> 3.37 us  [other_rep(): return lax.ppermute(block, 'rep', [(i, i ^ flip) for i in range(reps)])]
    ppermute x7 -> x8, starting transfers between devices: 21 us -> 25.6 us  [along_shard(): return lax.ppermute(block, 'shard', route)]
    pallas_call x3 -> x5, Pallas kernels: 14.5 us -> 17 us  [call(): pl.pallas_call(kernel, out_shape=[jax.ShapeDtypeStruct(shape, dtype) for...]
    unnamed x6 -> x16, local copies, waits for them, and re-layouts: 2.63 us -> 4.62 us
    pallas_call x1, Pallas kernels: 2.9 us -> 4.14 us  [local(): pl.pallas_call(prepare_kernel, out_shape=[jax.ShapeDtypeStruct((size, wid...]
    dynamic_update_slice x5 -> x0, local copies, waits for them, and re-layouts: 1.15 us -> none  [placed(): lax.dynamic_update_slice_in_dim(jnp.full((rows,), -1.0, F32), values, at, 0)]
  transfers between devices with their start and end apart: 16 -> 17, of which waited for: 5 -> 8; matrix products, arithmetic and copies ran while one was open for 2% -> 1% of each run, Pallas kernels for 12% -> 14%
where the time goes in v3:
time: 97.1 us; the launch traced here: 95.4 us
  starting transfers between devices  36.8 us (38%)
  waiting for transfers between devices  25.7 us (26%)
  Pallas kernels  21.2 us (22%)
  blocking collectives  6.35 us (7%)
  local copies, waits for them, and re-layouts  4.99 us (5%)
    ppermute x8, starting transfers between devices, along_shard(): return lax.ppermute(block, 'shard', route)  25.6 us
    ppermute x8, waiting for transfers between devices, along_shard(): return lax.ppermute(block, 'shard', route)  18.9 us
    pallas_call x5, Pallas kernels, call(): pl.pallas_call(kernel, out_shape=[jax.ShapeDtypeStruct(shape, dtype) for...  17 us
    ppermute x3, starting transfers between devices, partner(): return lax.ppermute(block, 'shard', [(i, i ^ 1) for i in range(shards)])  8.57 us
    pmax x1, blocking collectives, local(): return lax.pmax(best[0], 'rep')  6.35 us
    unnamed x16, local copies, waits for them, and re-layouts  4.62 us
    pallas_call x1, Pallas kernels, local(): pl.pallas_call(prepare_kernel, out_shape=[jax.ShapeDtypeStruct((size, wid...  4.14 us
    ppermute x3, waiting for transfers between devices, partner(): return lax.ppermute(block, 'shard', [(i, i ^ 1) for i in range(shards)])  3.44 us
  transfers between devices with their start and end apart: 17, of which 8 were waited for; matrix products, arithmetic and copies ran while one was open for 1% of the time, Pallas kernels for 14%

profile of v3, /device:TPU:8, one launch (start us, length us, event | category | flops | bytes accessed | tf_op | source)
XLA Modules:
  0.0 95.4 jit_solution(12126958900925059953)
XLA Ops:
  0.8 4.1 %prepare.1 = (bf16[256,1024]{1,0:T(8,128)(2,1)}, bf16[272,1024]{1,0:T(8,128)(2,1)S(1)}, bf16[256,1024]{1,0:T(8,128)(2,1)}, bf16[272,1024]{1,0:T(8,128)(2,1)S(1)}...) custom-call(s32[2]{0:T(128)S(1)} %pad_add_fusion.2.index_ref, bf16[2048,1024]{1,0:T(8,128)(2,1)} %emb_ref.1, ...), custom_call_target="tpu_custom_call" | custom-call | tf_op jit(solution)/shard_map/prepare/pallas_call | solution.py:206
  4.9 3.5 %collective-permute-start.2 = (bf16[272,1024]{1,0:T(8,128)(2,1)S(1)}, bf16[272,1024]{1,0:T(8,128)(2,1)S(1)}, u32[]{:S(2)}, u32[]{:S(2)}) collective-permute-start(bf16[272,1024]{1,0:T(8,128)(2,1)S(1)} %get-tuple-element.38.refs_5_.refs_9_), channel_id=1, source_target_pairs={{0,8},{4,12},{8,16},{12,20},{16,24},{20,28},{1,9},{5,13},{9,17},{1... | collective-permute-start | bytes 1671176 | tf_op jit(solution)/shard_map/ppermute | solution.py:183
  9.2 1.5 %collective-permute-start.3 = (bf16[272,1024]{1,0:T(8,128)(2,1)}, bf16[272,1024]{1,0:T(8,128)(2,1)S(1)}, u32[]{:S(2)}, u32[]{:S(2)}) collective-permute-start(bf16[272,1024]{1,0:T(8,128)(2,1)} %get-tuple-element.39), channel_id=1, source_target_pairs={{0,4},{4,0},{8,12},{12,8},{16,20},{20,16},{24,28},{28,24},{1,5},{5... | collective-permute-start | bytes 1671176 | tf_op jit(solution)/shard_map/ppermute | solution.py:186
  10.7 2.4 %collective-permute-start.4 = (bf16[272,1024]{1,0:T(8,128)(2,1)S(1)}, bf16[272,1024]{1,0:T(8,128)(2,1)S(1)}, u32[]{:S(2)}, u32[]{:S(2)}) collective-permute-start(bf16[272,1024]{1,0:T(8,128)(2,1)S(1)} %get-tuple-element.40), channel_id=1, source_target_pairs={{8,0},{12,4},{16,8},{20,12},{24,16},{28,20},{9,1},{13,5},{17,9},{2... | collective-permute-start | bytes 1671176 | tf_op jit(solution)/shard_map/ppermute | solution.py:183
  13.2 8.0 %collective-permute-done.2.refs_2_.refs_6_.refs_4_.refs_10_.refs_14_ = bf16[272,1024]{1,0:T(8,128)(2,1)S(1)} collective-permute-done((bf16[272,1024]{1,0:T(8,128)(2,1)S(1)}, bf16[272,1024]{1,0:T(8,128)(2,1)S(1)}, u32[]{:S(2)}, u32[]{:S(2)}) %collective-permute-start.2) | collective-permute-done | bytes 557088 | tf_op jit(solution)/shard_map/ppermute | solution.py:183
  21.2 2.4 %collective-permute-done.3.refs_0_.refs_7_.refs_11_.refs_15_ = bf16[272,1024]{1,0:T(8,128)(2,1)S(1)} collective-permute-done((bf16[272,1024]{1,0:T(8,128)(2,1)}, bf16[272,1024]{1,0:T(8,128)(2,1)S(1)}, u32[]{:S(2)}, u32[]{:S(2)}) %collective-permute-start.3) | collective-permute-done | bytes 557088 | tf_op jit(solution)/shard_map/ppermute | solution.py:186
  23.5 2.9 %collective-permute-done.4.refs_1_.refs_8_.refs_3_.refs_12_.refs_16_ = bf16[272,1024]{1,0:T(8,128)(2,1)S(1)} collective-permute-done((bf16[272,1024]{1,0:T(8,128)(2,1)S(1)}, bf16[272,1024]{1,0:T(8,128)(2,1)S(1)}, u32[]{:S(2)}, u32[]{:S(2)}) %collective-permute-start.4) | collective-permute-done | bytes 557088 | tf_op jit(solution)/shard_map/ppermute | solution.py:183
  26.4 1.5 %collective-permute-start.7 = (bf16[272,1024]{1,0:T(8,128)(2,1)S(1)}, bf16[272,1024]{1,0:T(8,128)(2,1)}, u32[]{:S(2)}, u32[]{:S(2)}) collective-permute-start(bf16[272,1024]{1,0:T(8,128)(2,1)S(1)} %collective-permute-done.2.refs_2_.refs_6_.refs_4_.refs_10_.refs_14_), channel_id=1, source_target_pairs={{0,2},{1,3},{2,0},{3,1},{4,6},{5,7},{6,4},{7,5},{8,10},{9,11},{10,... | collective-permute-start | bytes 1671176 | tf_op jit(solution)/shard_map/ppermute | solution.py:189
  27.9 3.5 %collective-permute-start = (bf16[256,1024]{1,0:T(8,128)(2,1)}, bf16[256,1024]{1,0:T(8,128)(2,1)}, u32[]{:S(2)}, u32[]{:S(2)}) collective-permute-start(bf16[256,1024]{1,0:T(8,128)(2,1)} %get-tuple-element.36), channel_id=1, source_target_pairs={{0,8},{4,12},{8,16},{12,20},{16,24},{20,28},{1,9},{5,13},{9,17},{1... | collective-permute-start | bytes 1572872 | tf_op jit(solution)/shard_map/ppermute | solution.py:183
  31.4 3.2 %collective-permute-start.1 = (bf16[256,1024]{1,0:T(8,128)(2,1)}, bf16[256,1024]{1,0:T(8,128)(2,1)}, u32[]{:S(2)}, u32[]{:S(2)}) collective-permute-start(bf16[256,1024]{1,0:T(8,128)(2,1)} %get-tuple-element.37), channel_id=1, source_target_pairs={{8,0},{12,4},{16,8},{20,12},{24,16},{28,20},{9,1},{13,5},{17,9},{2... | collective-permute-start | bytes 1572872 | tf_op jit(solution)/shard_map/ppermute | solution.py:183
  35.6 6.5 %own.1 = (bf16[2048,1024]{1,0:T(8,128)(2,1)S(1)}, f32[1,2048]{1,0:T(1,128)S(1)}) custom-call(s32[4]{0:T(128)S(1)} %pad_add_fusion.1.place_ref, bf16[2048,1024]{1,0:T(8,128)(2,1)} %emb_ref.1, s32[1,2048]{1,0:T(1,128)S(1)} %bitcast.11, s32[2048,1]{1,0:T(8,128)S(1)} %copy.3.row_labels_ref), custom_call_target="tpu_custom_call" | custom-call | flops 1024 | bytes 1024 | tf_op jit(solution)/shard_map/own/pallas_call | solution.py:192
  42.1 1.9 %copy-done = bf16[2048,1024]{1,0:T(8,128)(2,1)} copy-done((bf16[2048,1024]{1,0:T(8,128)(2,1)}, bf16[2048,1024]{1,0:T(8,128)(2,1)S(1)}, u32[]{:S(2)}) %copy-start) | copy-done | bytes 4194328
  44.0 2.8 %near.1 = (f32[1,2048]{1,0:T(1,128)S(1)}, f32[1,512]{1,0:T(1,128)S(1)}, f32[1,512]{1,0:T(1,128)S(1)}) custom-call(s32[4]{0:T(128)S(1)} %pad_add_fusion.1.place_ref, bf16[272,1024]{1,0:T(8,128)(2,1)S(1)} %collective-permute-done.3.refs_0_.refs_7_.refs_11_.refs_15_, bf16[272,1024]{1,0:T(8,128)(2,1)S(1)} %collective-permute-done.4.refs_1_.refs_8_.refs_3_.refs_12_.refs_16_, ...), custom_call_target="tpu_custom_call" | custom-call | flops 1024 | bytes 1024 | tf_op jit(solution)/shard_map/near/pallas_call | solution.py:192
  47.4 1.1 %collective-permute-done.5.refs_1_ = bf16[256,1024]{1,0:T(8,128)(2,1)} collective-permute-done((bf16[256,1024]{1,0:T(8,128)(2,1)}, bf16[256,1024]{1,0:T(8,128)(2,1)}, u32[]{:S(2)}, u32[]{:S(2)}) %collective-permute-start.5) | collective-permute-done | bytes 524320 | tf_op jit(solution)/shard_map/ppermute | solution.py:186
  49.0 3.3 %collective-permute-start.13 = (bf16[272,1024]{1,0:T(8,128)(2,1)S(1)}, bf16[272,1024]{1,0:T(8,128)(2,1)S(1)}, u32[]{:S(2)}, u32[]{:S(2)}) collective-permute-start(bf16[272,1024]{1,0:T(8,128)(2,1)S(1)} %collective-permute-done.4.refs_1_.refs_8_.refs_3_.refs_12_.refs_16_), channel_id=1, source_target_pairs={{0,4},{8,12},{16,20},{24,28},{1,5},{9,13},{17,21},{25,29},{2,6},{1... | collective-permute-start | bytes 1671176 | tf_op jit(solution)/shard_map/ppermute | solution.py:183
  53.7 4.3 %next.1 = (f32[1,2048]{1,0:T(1,128)S(1)}, f32[1,512]{1,0:T(1,128)S(1)}, f32[1,512]{1,0:T(1,128)S(1)}) custom-call(s32[4]{0:T(128)S(1)} %pad_add_fusion.1.place_ref, bf16[272,1024]{1,0:T(8,128)(2,1)S(1)} %collective-permute-done.3.refs_0_.refs_7_.refs_11_.refs_15_, bf16[256,1024]{1,0:T(8,128)(2,1)} %collective-permute-done.5.refs_1_, ...), custom_call_target="tpu_custom_call" | custom-call | flops 1024 | bytes 1024 | tf_op jit(solution)/shard_map/next/pallas_call | solution.py:192
  57.9 3.4 %collective-permute-done.9.refs_9_ = bf16[256,1024]{1,0:T(8,128)(2,1)S(1)} collective-permute-done((bf16[256,1024]{1,0:T(8,128)(2,1)}, bf16[256,1024]{1,0:T(8,128)(2,1)S(1)}, u32[]{:S(2)}, u32[]{:S(2)}) %collective-permute-start.9) | collective-permute-done | bytes 524320 | tf_op jit(solution)/shard_map/ppermute | solution.py:189
  61.3 2.4 %collective-permute-done.13.refs_13_.refs_17_ = bf16[272,1024]{1,0:T(8,128)(2,1)S(1)} collective-permute-done((bf16[272,1024]{1,0:T(8,128)(2,1)S(1)}, bf16[272,1024]{1,0:T(8,128)(2,1)S(1)}, u32[]{:S(2)}, u32[]{:S(2)}) %collective-permute-start.13) | collective-permute-done | bytes 557088 | tf_op jit(solution)/shard_map/ppermute | solution.py:183
  64.9 2.9 %far.1 = (f32[1,512]{1,0:T(1,128)S(1)}, f32[1,512]{1,0:T(1,128)S(1)}, f32[1,512]{1,0:T(1,128)S(1)}) custom-call(s32[4]{0:T(128)S(1)} %pad_add_fusion.1.place_ref, bf16[272,1024]{1,0:T(8,128)(2,1)S(1)} %collective-permute-done.3.refs_0_.refs_7_.refs_11_.refs_15_, bf16[256,1024]{1,0:T(8,128)(2,1)} %collective-permute-done.5.refs_1_, ...), custom_call_target="tpu_custom_call" | custom-call | flops 1024 | bytes 1024 | tf_op jit(solution)/shard_map/far/pallas_call | solution.py:192
  67.8 6.5 %collective-permute-start.14 = (f32[1,512]{1,0:T(1,128)S(1)}, f32[1,512]{1,0:T(1,128)S(1)}, u32[]{:S(2)}, u32[]{:S(2)}) collective-permute-start(f32[1,512]{1,0:T(1,128)S(1)} %get-tuple-element.64), channel_id=1, source_target_pairs={{0,4},{4,0},{8,12},{12,8},{16,20},{20,16},{24,28},{28,24},{1,5},{5... | collective-permute-start | bytes 6152 | tf_op jit(solution)/shard_map/ppermute | solution.py:186
  74.3 7.8 %collective-permute-start.15 = (f32[1,512]{1,0:T(1,128)S(1)}, f32[1,512]{1,0:T(1,128)S(1)}, u32[]{:S(2)}, u32[]{:S(2)}) collective-permute-start(f32[1,512]{1,0:T(1,128)S(1)} %get-tuple-element.65), channel_id=1, source_target_pairs={{0,8},{4,12},{8,16},{12,20},{16,24},{20,28},{1,9},{5,13},{9,17},{1... | collective-permute-start | bytes 6152 | tf_op jit(solution)/shard_map/ppermute | solution.py:183
  82.1 1.3 %collective-permute-start.16 = (f32[1,512]{1,0:T(1,128)S(1)}, f32[1,512]{1,0:T(1,128)S(1)}, u32[]{:S(2)}, u32[]{:S(2)}) collective-permute-start(f32[1,512]{1,0:T(1,128)S(1)} %get-tuple-element.66), channel_id=1, source_target_pairs={{4,8},{12,16},{20,24},{5,9},{13,17},{21,25},{6,10},{14,18},{22,26}... | collective-permute-start | bytes 6152 | tf_op jit(solution)/shard_map/ppermute | solution.py:183
  83.5 5.0 %collective-permute-done.16.beside_ref = f32[1,512]{1,0:T(1,128)S(1)} collective-permute-done((f32[1,512]{1,0:T(1,128)S(1)}, f32[1,512]{1,0:T(1,128)S(1)}, u32[]{:S(2)}, u32[]{:S(2)}) %collective-permute-start.16) | collective-permute-done | bytes 2080 | tf_op jit(solution)/shard_map/ppermute | solution.py:183
  89.1 6.3 %pmax.7 = f32[2048]{0:T(1024)} all-reduce(f32[2048]{0:T(1024)S(1)} %bitcast.12), channel_id=1, replica_groups=mesh['shard'=8,'rep'=4] {'rep'}, use_global_device_ids=true, to_apply=%region_0.1 | all-reduce | flops 2048 | bytes 16384 | tf_op jit(solution)/shard_map/pmax | solution.py:308
  (37 shorter events, 6.9 us)
Async XLA Ops:
  0.8 34.4 %copy-start.4 = (s32[2048]{0:T(1024)S(1)}, s32[2048]{0:T(1024)}, u32[]{:S(2)}) copy-start(s32[2048]{0:T(1024)} %param.3) | copy-start | bytes 24580
  4.9 16.2 %collective-permute-start.2 = (bf16[272,1024]{1,0:T(8,128)(2,1)S(1)}, bf16[272,1024]{1,0:T(8,128)(2,1)S(1)}, u32[]{:S(2)}, u32[]{:S(2)}) collective-permute-start(bf16[272,1024]{1,0:T(8,128)(2,1)S(1)} %get-tuple-element.38.refs_5_.refs_9_), channel_id=1, source_target_pairs={{0,8},{4,12},{8,16},{12,20},{16,24},{20,28},{1,9},{5,13},{9,17},{1... | collective-permute-start | bytes 1671176 | tf_op jit(solution)/shard_map/ppermute | solution.py:183
  8.4 0.8 copy-start.1
  9.2 14.3 %collective-permute-start.3 = (bf16[272,1024]{1,0:T(8,128)(2,1)}, bf16[272,1024]{1,0:T(8,128)(2,1)S(1)}, u32[]{:S(2)}, u32[]{:S(2)}) collective-permute-start(bf16[272,1024]{1,0:T(8,128)(2,1)} %get-tuple-element.39), channel_id=1, source_target_pairs={{0,4},{4,0},{8,12},{12,8},{16,20},{20,16},{24,28},{28,24},{1,5},{5... | collective-permute-start | bytes 1671176 | tf_op jit(solution)/shard_map/ppermute | solution.py:186
  10.7 15.7 %collective-permute-start.4 = (bf16[272,1024]{1,0:T(8,128)(2,1)S(1)}, bf16[272,1024]{1,0:T(8,128)(2,1)S(1)}, u32[]{:S(2)}, u32[]{:S(2)}) collective-permute-start(bf16[272,1024]{1,0:T(8,128)(2,1)S(1)} %get-tuple-element.40), channel_id=1, source_target_pairs={{8,0},{12,4},{16,8},{20,12},{24,16},{28,20},{9,1},{13,5},{17,9},{2... | collective-permute-start | bytes 1671176 | tf_op jit(solution)/shard_map/ppermute | solution.py:183
  26.4 17.6 %collective-permute-start.6 = (bf16[272,1024]{1,0:T(8,128)(2,1)S(1)}, bf16[272,1024]{1,0:T(8,128)(2,1)S(1)}, u32[]{:S(2)}, u32[]{:S(2)}) collective-permute-start(bf16[272,1024]{1,0:T(8,128)(2,1)S(1)} %collective-permute-done.2.refs_2_.refs_6_.refs_4_.refs_10_.refs_14_), channel_id=1, source_target_pairs={{0,1},{1,0},{2,3},{3,2},{4,5},{5,4},{6,7},{7,6},{8,9},{9,8},{10,11... | collective-permute-start | bytes 1671176 | tf_op jit(solution)/shard_map/ppermute | solution.py:189
  26.4 22.1 %collective-permute-start.7 = (bf16[272,1024]{1,0:T(8,128)(2,1)S(1)}, bf16[272,1024]{1,0:T(8,128)(2,1)}, u32[]{:S(2)}, u32[]{:S(2)}) collective-permute-start(bf16[272,1024]{1,0:T(8,128)(2,1)S(1)} %collective-permute-done.2.refs_2_.refs_6_.refs_4_.refs_10_.refs_14_), channel_id=1, source_target_pairs={{0,2},{1,3},{2,0},{3,1},{4,6},{5,7},{6,4},{7,5},{8,10},{9,11},{10,... | collective-permute-start | bytes 1671176 | tf_op jit(solution)/shard_map/ppermute | solution.py:189
  27.9 18.9 %collective-permute-start = (bf16[256,1024]{1,0:T(8,128)(2,1)}, bf16[256,1024]{1,0:T(8,128)(2,1)}, u32[]{:S(2)}, u32[]{:S(2)}) collective-permute-start(bf16[256,1024]{1,0:T(8,128)(2,1)} %get-tuple-element.36), channel_id=1, source_target_pairs={{0,8},{4,12},{8,16},{12,20},{16,24},{20,28},{1,9},{5,13},{9,17},{1... | collective-permute-start | bytes 1572872 | tf_op jit(solution)/shard_map/ppermute | solution.py:183
  31.4 16.0 %collective-permute-start.1 = (bf16[256,1024]{1,0:T(8,128)(2,1)}, bf16[256,1024]{1,0:T(8,128)(2,1)}, u32[]{:S(2)}, u32[]{:S(2)}) collective-permute-start(bf16[256,1024]{1,0:T(8,128)(2,1)} %get-tuple-element.37), channel_id=1, source_target_pairs={{8,0},{12,4},{16,8},{20,12},{24,16},{28,20},{9,1},{13,5},{17,9},{2... | collective-permute-start | bytes 1572872 | tf_op jit(solution)/shard_map/ppermute | solution.py:183
  34.6 13.9 %collective-permute-start.5 = (bf16[256,1024]{1,0:T(8,128)(2,1)}, bf16[256,1024]{1,0:T(8,128)(2,1)}, u32[]{:S(2)}, u32[]{:S(2)}) collective-permute-start(bf16[256,1024]{1,0:T(8,128)(2,1)} %get-tuple-element.42), channel_id=1, source_target_pairs={{0,4},{4,0},{8,12},{12,8},{16,20},{20,16},{24,28},{28,24},{1,5},{5... | collective-permute-start | bytes 1572872 | tf_op jit(solution)/shard_map/ppermute | solution.py:186
  35.5 8.5 %copy-start.2 = (bf16[272,1024]{1,0:T(8,128)(2,1)S(1)}, bf16[272,1024]{1,0:T(8,128)(2,1)}, u32[]{:S(2)}) copy-start(bf16[272,1024]{1,0:T(8,128)(2,1)} %copy-done.1) | copy-start | bytes 1671172
  42.0 2.0 %copy-start = (bf16[2048,1024]{1,0:T(8,128)(2,1)}, bf16[2048,1024]{1,0:T(8,128)(2,1)S(1)}, u32[]{:S(2)}) copy-start(bf16[2048,1024]{1,0:T(8,128)(2,1)S(1)} %get-tuple-element.47.refs_4_.refs_8_) | copy-start | bytes 12582916
  48.5 12.8 %collective-permute-start.9 = (bf16[256,1024]{1,0:T(8,128)(2,1)}, bf16[256,1024]{1,0:T(8,128)(2,1)S(1)}, u32[]{:S(2)}, u32[]{:S(2)}) collective-permute-start(bf16[256,1024]{1,0:T(8,128)(2,1)} %collective-permute-done.refs_5_), channel_id=1, source_target_pairs={{0,2},{1,3},{2,0},{3,1},{4,6},{5,7},{6,4},{7,5},{8,10},{9,11},{10,... | collective-permute-start | bytes 1572872 | tf_op jit(solution)/shard_map/ppermute | solution.py:189
  49.0 14.7 %collective-permute-start.13 = (bf16[272,1024]{1,0:T(8,128)(2,1)S(1)}, bf16[272,1024]{1,0:T(8,128)(2,1)S(1)}, u32[]{:S(2)}, u32[]{:S(2)}) collective-permute-start(bf16[272,1024]{1,0:T(8,128)(2,1)S(1)} %collective-permute-done.4.refs_1_.refs_8_.refs_3_.refs_12_.refs_16_), channel_id=1, source_target_pairs={{0,4},{8,12},{16,20},{24,28},{1,5},{9,13},{17,21},{25,29},{2,6},{1... | collective-permute-start | bytes 1671176 | tf_op jit(solution)/shard_map/ppermute | solution.py:183
  52.3 11.4 %collective-permute-start.10 = (bf16[272,1024]{1,0:T(8,128)(2,1)}, bf16[272,1024]{1,0:T(8,128)(2,1)S(1)}, u32[]{:S(2)}, u32[]{:S(2)}) collective-permute-start(bf16[272,1024]{1,0:T(8,128)(2,1)} %collective-permute-done.7.refs_7_.refs_8_), channel_id=1, source_target_pairs={{0,1},{1,0},{2,3},{3,2},{4,5},{5,4},{6,7},{7,6},{8,9},{9,8},{10,11... | collective-permute-start | bytes 1671176 | tf_op jit(solution)/shard_map/ppermute | solution.py:189
  52.4 11.3 %collective-permute-start.12 = (bf16[272,1024]{1,0:T(8,128)(2,1)S(1)}, bf16[272,1024]{1,0:T(8,128)(2,1)S(1)}, u32[]{:S(2)}, u32[]{:S(2)}) collective-permute-start(bf16[272,1024]{1,0:T(8,128)(2,1)S(1)} %collective-permute-done.3.refs_0_.refs_7_.refs_11_.refs_15_), channel_id=1, source_target_pairs={{12,4},{20,12},{28,20},{13,5},{21,13},{29,21},{14,6},{22,14},{30,2... | collective-permute-start | bytes 1671176 | tf_op jit(solution)/shard_map/ppermute | solution.py:183
  53.1 10.6 %collective-permute-start.8 = (bf16[256,1024]{1,0:T(8,128)(2,1)}, bf16[256,1024]{1,0:T(8,128)(2,1)S(1)}, u32[]{:S(2)}, u32[]{:S(2)}) collective-permute-start(bf16[256,1024]{1,0:T(8,128)(2,1)} %collective-permute-done.refs_5_), channel_id=1, source_target_pairs={{0,1},{1,0},{2,3},{3,2},{4,5},{5,4},{6,7},{7,6},{8,9},{9,8},{10,11... | collective-permute-start | bytes 1572872 | tf_op jit(solution)/shard_map/ppermute | solution.py:189
  61.3 2.4 %collective-permute-start.11 = (bf16[256,1024]{1,0:T(8,128)(2,1)S(1)}, bf16[256,1024]{1,0:T(8,128)(2,1)S(1)}, u32[]{:S(2)}, u32[]{:S(2)}) collective-permute-start(bf16[256,1024]{1,0:T(8,128)(2,1)S(1)} %collective-permute-done.9.refs_9_), channel_id=1, source_target_pairs={{0,1},{1,0},{2,3},{3,2},{4,5},{5,4},{6,7},{7,6},{8,9},{9,8},{10,11... | collective-permute-start | bytes 1572872 | tf_op jit(solution)/shard_map/ppermute | solution.py:189
  63.7 0.8 copy-start.5
  63.7 1.0 %copy-start.6 = (bf16[272,1024]{1,0:T(8,128)(2,1)}, bf16[272,1024]{1,0:T(8,128)(2,1)S(1)}, u32[]{:S(2)}) copy-start(bf16[272,1024]{1,0:T(8,128)(2,1)S(1)} %collective-permute-done.10.refs_10_) | copy-start | bytes 1671172
  63.7 1.2 %copy-start.7 = (bf16[272,1024]{1,0:T(8,128)(2,1)}, bf16[272,1024]{1,0:T(8,128)(2,1)S(1)}, u32[]{:S(2)}) copy-start(bf16[272,1024]{1,0:T(8,128)(2,1)S(1)} %collective-permute-done.12.refs_12_) | copy-start | bytes 1671172
  67.8 15.7 %collective-permute-start.14 = (f32[1,512]{1,0:T(1,128)S(1)}, f32[1,512]{1,0:T(1,128)S(1)}, u32[]{:S(2)}, u32[]{:S(2)}) collective-permute-start(f32[1,512]{1,0:T(1,128)S(1)} %get-tuple-element.64), channel_id=1, source_target_pairs={{0,4},{4,0},{8,12},{12,8},{16,20},{20,16},{24,28},{28,24},{1,5},{5... | collective-permute-start | bytes 6152 | tf_op jit(solution)/shard_map/ppermute | solution.py:186
  74.3 9.2 %collective-permute-start.15 = (f32[1,512]{1,0:T(1,128)S(1)}, f32[1,512]{1,0:T(1,128)S(1)}, u32[]{:S(2)}, u32[]{:S(2)}) collective-permute-start(f32[1,512]{1,0:T(1,128)S(1)} %get-tuple-element.65), channel_id=1, source_target_pairs={{0,8},{4,12},{8,16},{12,20},{16,24},{20,28},{1,9},{5,13},{9,17},{1... | collective-permute-start | bytes 6152 | tf_op jit(solution)/shard_map/ppermute | solution.py:183
  82.1 6.4 %collective-permute-start.16 = (f32[1,512]{1,0:T(1,128)S(1)}, f32[1,512]{1,0:T(1,128)S(1)}, u32[]{:S(2)}, u32[]{:S(2)}) collective-permute-start(f32[1,512]{1,0:T(1,128)S(1)} %get-tuple-element.66), channel_id=1, source_target_pairs={{4,8},{12,16},{20,24},{5,9},{13,17},{21,25},{6,10},{14,18},{22,26}... | collective-permute-start | bytes 6152 | tf_op jit(solution)/shard_map/ppermute | solution.py:183
  (1 other events, 0.7 us)

commit v4 on v0

v4 whole, which is shorter than its diff:
```python
import functools
import math

import jax
import jax.numpy as jnp
from jax import lax
from jax.experimental import pallas as pl
from jax.experimental.pallas import tpu as pltpu
from jax.sharding import PartitionSpec as P

F32 = jnp.float32
BF16 = jnp.bfloat16
LOOK = 4
TILE = 256
WIDE = 512
INFO = 16
VMEM_LIMIT = 32 * 1024 * 1024
VMEM = pl.BlockSpec(memory_space=pltpu.VMEM)
SMEM = pl.BlockSpec(memory_space=pltpu.SMEM)


def normalize(values):
    as_float = values.astype(F32)
    inverse = lax.rsqrt(jnp.mean(as_float * as_float, axis=1, keepdims=True) + 1e-06)
    return (as_float * inverse / math.sqrt(values.shape[1])).astype(BF16)


def score(keys, queries):
    return lax.dot_general(keys, queries, (((1,), (1,)), ((), ())), preferred_element_type=F32)


def fold(values):
    rows, cols = values.shape
    return jnp.max(values.reshape(rows // 8, 8, cols), axis=0)


def prepare_kernel(index_ref, mine_ref, labels_ref, lo_out, hi_out):
    labels = labels_ref[...]
    first, last = jnp.min(labels), jnp.max(labels)
    head = jnp.sum((labels == first).astype(jnp.int32))
    tail = jnp.sum((labels == last).astype(jnp.int32))
    row = lax.broadcasted_iota(jnp.int32, (INFO, mine_ref.shape[1]), 0)
    info = jnp.zeros(row.shape, jnp.int32)
    for n, value in enumerate([first, head // 16, head % 16, last, tail // 16, tail % 16]):
        info = jnp.where(row == n, value, info)
    half = hi_out.shape[0]
    for n in range(half // 128):
        at = pl.ds(n * 128, 128)
        lo_out[at, :] = normalize(mine_ref[at, :])
        hi_out[at, :] = normalize(mine_ref[pl.ds(half + n * 128, 128), :])
    lo_out[pl.ds(half, INFO), :] = info.astype(F32).astype(BF16)


def read_reach(ref, at):
    block = ref[pl.ds(ref.shape[0] - INFO, INFO), pl.ds(0, 128)].astype(F32)
    packed = block[at : at + 1] + 256.0 * (16.0 * block[at + 1 : at + 2] + block[at + 2 : at + 3])
    packed = jnp.max(packed).astype(jnp.int32)
    return packed % 256, packed // 256


def own_kernel(place_ref, emb_ref, labels_ref, row_labels_ref, own_out, best_out, reach_out):
    rows = emb_ref.shape[0]
    labels = labels_ref[...]
    first = jnp.min(labels)
    reach_out[0] = first
    reach_out[1] = jnp.sum((labels == first).astype(jnp.int32))
    for n in range(rows // 128):
        own_out[pl.ds(n * 128, 128), :] = normalize(emb_ref[pl.ds(n * 128, 128), :])
    best_out[...] = jnp.full(best_out.shape, -1.0, F32)
    for n in range(2):
        tile = place_ref[0] if n == 0 else rows // TILE - 1 - place_ref[0]
        at = pl.multiple_of(tile * TILE, TILE)
        keys = own_out[pl.ds(at, TILE), :]
        row_labels = row_labels_ref[pl.ds(at, TILE), :]

        def over_queries(j, _):
            cols = pl.ds(pl.multiple_of(j * WIDE, WIDE), WIDE)
            scores = score(keys, own_out[cols, :])
            row = lax.broadcasted_iota(jnp.int32, scores.shape, 0) + at
            col = lax.broadcasted_iota(jnp.int32, scores.shape, 1) + j * WIDE
            keep = (row_labels == labels_ref[:, cols]) & (row < col)
            best = jnp.max(fold(jnp.where(keep, scores, -1.0)), axis=0, keepdims=True)
            best_out[:, cols] = jnp.maximum(best_out[:, cols], best)
            return 0

        lax.fori_loop(at // WIDE, rows // WIDE, over_queries, 0)


def earlier_kernel(fresh, base, place_ref, own_reach, own_ref, best_ref, keys_ref, *refs):
    reach_in, (best_out, reach_out) = (None, refs) if fresh else (refs[0], refs[1:])
    step = pl.program_id(0)
    rows, half = own_ref.shape[0], TILE

    @pl.when(step == 0)
    def _():
        best_out[...] = best_ref[...]

    if fresh:
        label, tail = read_reach(keys_ref, 3)
        reach_out[2 * step], reach_out[2 * step + 1] = label, tail
    else:
        label, tail = reach_in[2 * step], reach_in[2 * step + 1]
        reach_out[2 * step], reach_out[2 * step + 1] = label, tail
    count = jnp.where((place_ref[step] >= 0) & (label == own_reach[0]), own_reach[1], 0)
    first = rows - tail - place_ref[LOOK] * 2 * half - base
    count = jnp.where(first < half, count, 0)

    def over_queries(j, _):
        at = pl.multiple_of(j * WIDE, WIDE)
        scores = score(keys_ref[pl.ds(0, half), :], own_ref[pl.ds(at, WIDE), :])
        index = lax.broadcasted_iota(jnp.int32, scores.shape, 0)
        best = jnp.max(fold(jnp.where(index >= first, scores, -1.0)), axis=0, keepdims=True)
        col = lax.broadcasted_iota(jnp.int32, best.shape, 1) + at
        cols = pl.ds(at, WIDE)
        best_out[:, cols] = jnp.maximum(best_out[:, cols], jnp.where(col < count, best, -1.0))
        return 0

    lax.fori_loop(0, (count + WIDE - 1) // WIDE, over_queries, 0)


def local(embeddings, labels):
    rows, width = embeddings.shape
    shards, reps = lax.axis_size("shard"), lax.axis_size("rep")
    s, r = lax.axis_index("shard"), lax.axis_index("rep")
    quarter = rows // reps
    half = quarter // 2
    params = pltpu.CompilerParams(vmem_limit_bytes=VMEM_LIMIT)
    streamed = pltpu.CompilerParams(vmem_limit_bytes=60 * 1024 * 1024)
    small = pl.CostEstimate(flops=1024, bytes_accessed=1024, transcendentals=0)

    sizes = [half + INFO, half]
    lo, hi = pl.pallas_call(
        prepare_kernel,
        out_shape=[jax.ShapeDtypeStruct((size, width), BF16) for size in sizes],
        grid_spec=pltpu.PrefetchScalarGridSpec(
            num_scalar_prefetch=1,
            grid=(1,),
            in_specs=[
                pl.BlockSpec((quarter, width), lambda i, at: (at[0], 0)),
                pl.BlockSpec((rows // 128, 128), lambda i, at: (0, 0)),
            ],
            out_specs=[pl.BlockSpec((size, width), lambda i, at: (0, 0)) for size in sizes],
        ),
        compiler_params=streamed,
        name="prepare",
    )(r[None].astype(jnp.int32), embeddings, labels.reshape(rows // 128, 128))

    whole = shards <= 2 * LOOK

    def earlier(piece):
        if whole:
            return lax.all_gather(piece, "shard")
        pieces = [
            lax.ppermute(piece, "shard", [(i, i + n) for i in range(shards - n)])
            for n in range(1, LOOK + 1)
        ]
        return jnp.stack(pieces)

    lo_all, hi_all = earlier(lo), earlier(hi)

    own, best, own_reach = pl.pallas_call(
        own_kernel,
        out_shape=[
            jax.ShapeDtypeStruct((rows, width), BF16),
            jax.ShapeDtypeStruct((1, rows), F32),
            jax.ShapeDtypeStruct((2,), jnp.int32),
        ],
        in_specs=[SMEM, VMEM, VMEM, VMEM],
        out_specs=[VMEM, VMEM, SMEM],
        compiler_params=params,
        cost_estimate=small,
        name="own",
    )(r[None].astype(jnp.int32), embeddings, labels[None, :], labels[:, None])

    shard_of = s - 1 - jnp.arange(LOOK, dtype=jnp.int32)
    place = jnp.concatenate([shard_of, r[None]]).astype(jnp.int32)

    def against(pieces, best, reach):
        size = pieces.shape[1]
        which = lambda i, at: (jnp.maximum(at[i], 0) if whole else i, 0, 0)
        full = pl.BlockSpec((rows, width), lambda i, at: (0, 0))
        line = pl.BlockSpec((1, rows), lambda i, at: (0, 0))
        fresh = reach is None
        return pl.pallas_call(
            functools.partial(earlier_kernel, fresh, 0 if fresh else half),
            out_shape=[
                jax.ShapeDtypeStruct((1, rows), F32),
                jax.ShapeDtypeStruct((2 * LOOK,), jnp.int32),
            ],
            grid_spec=pltpu.PrefetchScalarGridSpec(
                num_scalar_prefetch=1,
                grid=(LOOK,),
                in_specs=[SMEM, full, line, pl.BlockSpec((None, size, width), which)]
                + ([] if fresh else [SMEM]),
                out_specs=[line, SMEM],
            ),
            compiler_params=streamed,
            cost_estimate=small,
            name="earlier",
        )(place, own_reach, own, best, pieces, *([] if fresh else [reach]))

    best, reach = against(lo_all, best, None)
    best, _ = against(hi_all, best, reach)
    return lax.pmax(best[0], "rep")


def solution(mesh):
    placed = (P("shard", None), P("shard"))
    return jax.shard_map(local, mesh=mesh, in_specs=placed, out_specs=P("shard"), check_vma=False)
```

time: 170 us -> 184 us (1.082)
  the two profiles are of different devices: /device:TPU:18 before, /device:TPU:8 now
where the time goes in v4:
time: 184 us; the launch traced here: 182 us
  waiting for transfers between devices  134 us (73%)
  Pallas kernels  21.8 us (12%)
  between operations  13.5 us (7%)
  blocking collectives  6.47 us (4%)
  local copies, waits for them, and re-layouts  5.67 us (3%)
    all_gather x2, waiting for transfers between devices, earlier(): return lax.all_gather(piece, 'shard')  133 us
    pallas_call x2, Pallas kernels, against(): pl.pallas_call(functools.partial(earlier_kernel, fresh, 0 if fresh else h...  14.2 us
    pmax x1, blocking collectives, local(): return lax.pmax(best[0], 'rep')  6.47 us
    unnamed x10, local copies, waits for them, and re-layouts  5.3 us
    pallas_call x1, Pallas kernels, local(): pl.pallas_call(own_kernel, out_shape=[jax.ShapeDtypeStruct((rows, width),...  4.86 us
  transfers between devices with their start and end apart: 2, of which 2 were waited for; matrix products, arithmetic and copies ran while one was open for 1% of the time, Pallas kernels for 6%

profile of v4, /device:TPU:8, one launch (start us, length us, event | category | flops | bytes accessed | tf_op | source)
XLA Modules:
  0.0 181.6 jit_solution(6779512675463469996)
XLA Ops:
  6.5 0.0 copy-start.2
  6.5 0.0 all-gather.5.cloned.1.call-start
  6.5 2.7 %prepare.1 = (bf16[272,1024]{1,0:T(8,128)(2,1)}, bf16[256,1024]{1,0:T(8,128)(2,1)}) custom-call(s32[1]{0:T(128)} %bitcast.place_ref.index_ref, bf16[2048,1024]{1,0:T(8,128)(2,1)} %mine_ref.1, s32[16,128]{1,0:T(8,128)} %bitcast.7), custom_call_target="tpu_custom_call" | custom-call | tf_op jit(solution)/shard_map/prepare/pallas_call | solution.py:132
  9.3 0.0 all-gather.5.cloned.1.call-update
  9.3 0.0 all-gather.7.cloned.1.call-start
  9.3 0.7 all-gather.7.cloned.1.call-update
  10.1 0.0 copy-done.2
  10.1 0.4 copy.3.row_labels_ref
  10.4 0.0 copy-start
  10.4 2.2 %copy-done = bf16[2048,1024]{1,0:T(8,128)(2,1)S(1)} copy-done((bf16[2048,1024]{1,0:T(8,128)(2,1)S(1)}, bf16[2048,1024]{1,0:T(8,128)(2,1)}, u32[]{:S(2)}) %copy-start) | copy-done | bytes 4194328
  12.6 4.9 %own.1 = (bf16[2048,1024]{1,0:T(8,128)(2,1)S(1)}, f32[1,2048]{1,0:T(1,128)S(1)}, s32[2]{0:T(128)S(1)}) custom-call(s32[1]{0:T(128)} %bitcast.place_ref.index_ref, bf16[2048,1024]{1,0:T(8,128)(2,1)S(1)} %copy-done, s32[1,2048]{1,0:T(1,128)S(1)} %bitcast.9, s32[2048,1]{1,0:T(8,128)S(1)} %copy.3.row_labels_ref), custom_call_target="tpu_custom_call" | custom-call | flops 1024 | bytes 1024 | tf_op jit(solution)/shard_map/own/pallas_call | solution.py:161
  17.5 0.0 copy-start.1
  17.5 2.0 %copy-done.1 = bf16[2048,1024]{1,0:T(8,128)(2,1)} copy-done((bf16[2048,1024]{1,0:T(8,128)(2,1)}, bf16[2048,1024]{1,0:T(8,128)(2,1)S(1)}, u32[]{:S(2)}) %copy-start.1) | copy-done | bytes 4194328
  19.5 0.0 copy-start.3
  19.5 0.6 copy-done.3
  20.1 0.0 copy-start.4
  20.1 0.5 copy-done.4
  20.6 0.6 pad_add_fusion.place_ref
  21.2 65.4 %all-gather.5.cloned.1.call-done = bf16[2176,1024]{1,0:T(8,128)(2,1)} async-done(((bf16[272,1024]{1,0:T(8,128)(2,1)}), bf16[2176,1024]{1,0:T(8,128)(2,1)}) %all-gather.5.cloned.1.call-update) | async-done | bytes 4456464 | tf_op jit(solution)/shard_map/all_gather | solution.py:152
  86.6 6.4 %earlier.2 = (f32[1,2048]{1,0:T(1,128)}, s32[8]{0:T(128)}) custom-call(s32[5]{0:T(128)} %pad_add_fusion.place_ref, s32[2]{0:T(128)} %copy-done.4, bf16[2048,1024]{1,0:T(8,128)(2,1)} %copy-done.1, f32[1,2048]{1,0:T(1,128)} %copy-done.3, bf16[8,272,1024]{2,1,0:T(8,128)(2,1)} %bitcast.10), custom_call_target="tpu_custom_call" | custom-call | flops 1024 | bytes 1024 | tf_op jit(solution)/shard_map/earlier/pallas_call | solution.py:184
  92.9 67.5 %all-gather.7.cloned.1.call-done = bf16[2048,1024]{1,0:T(8,128)(2,1)} async-done(((bf16[256,1024]{1,0:T(8,128)(2,1)}), bf16[2048,1024]{1,0:T(8,128)(2,1)}) %all-gather.7.cloned.1.call-update) | async-done | bytes 4194320 | tf_op jit(solution)/shard_map/all_gather | solution.py:152
  160.5 7.8 %earlier.3 = (f32[1,2048]{1,0:T(1,128)}, s32[8]{0:T(128)}) custom-call(s32[5]{0:T(128)} %pad_add_fusion.place_ref, s32[2]{0:T(128)} %copy-done.4, bf16[2048,1024]{1,0:T(8,128)(2,1)} %copy-done.1, f32[1,2048]{1,0:T(1,128)} %get-tuple-element.17.best_ref, bf16[8,256,1024]{2,1,0:T(8,128)(2,1)} %bitcast.11, s32[8]{0:T(128)} %get-tuple-element.19.refs_0_), custom_call_target="tpu_custom_call" | custom-call | flops 1024 | bytes 1024 | tf_op jit(solution)/shard_map/earlier/pallas_call | solution.py:184
  168.3 6.5 %pmax.7 = f32[2048]{0:T(1024)} all-reduce(f32[2048]{0:T(1024)} %bitcast.12), channel_id=1, replica_groups=mesh['shard'=8,'rep'=4] {'rep'}, use_global_device_ids=true, to_apply=%region_0.0 | all-reduce | flops 2048 | bytes 16384 | tf_op jit(solution)/shard_map/pmax | solution.py:204
  (1 shorter events, 0.0 us)
Async XLA Ops:
  6.5 3.5 %copy-start.2 = (s32[2048]{0:T(1024)S(1)}, s32[2048]{0:T(1024)}, u32[]{:S(2)}) copy-start(s32[2048]{0:T(1024)} %param.3) | copy-start | bytes 24580
  6.5 80.0 %all-gather.5.cloned.1.call-start = ((), (), s32[]{:S(2)}) async-start(), calls=%async_computation | async-start | bytes 5013504 | tf_op jit(solution)/shard_map/all_gather | solution.py:152
  9.3 151.2 %all-gather.7.cloned.1.call-start = ((), (), s32[]{:S(2)}) async-start(), calls=%async_computation.1 | async-start | bytes 4718592 | tf_op jit(solution)/shard_map/all_gather | solution.py:152
  10.4 2.2 %copy-start = (bf16[2048,1024]{1,0:T(8,128)(2,1)S(1)}, bf16[2048,1024]{1,0:T(8,128)(2,1)}, u32[]{:S(2)}) copy-start(bf16[2048,1024]{1,0:T(8,128)(2,1)} %mine_ref.1) | copy-start | bytes 12582916
  17.5 2.0 %copy-start.1 = (bf16[2048,1024]{1,0:T(8,128)(2,1)}, bf16[2048,1024]{1,0:T(8,128)(2,1)S(1)}, u32[]{:S(2)}) copy-start(bf16[2048,1024]{1,0:T(8,128)(2,1)S(1)} %get-tuple-element.14.own_ref) | copy-start | bytes 12582916
  19.5 0.6 copy-start.3
  20.1 0.5 copy-start.4
Sparse Core Ops, SparseCore 0:
  9.5 76.9 all-gather.4
  88.7 71.7 all-gather.6
